TPU v7x, 32 devices: a whole 2x2x4 slice. The times are simulated.
32 devices in a mesh: blk: 16 (over z, y, core), across: 2 (over x).
Axes of the slice: x: 2, y: 2, z: 4, core: 2. Of those that a mesh axis runs over, the one named last changes fastest.
Arguments:
- positions: float32 [3, 262144], P(None, ('blk', 'across')), may hold values from -4 to 4
- strengths: float32 [3, 262144], P(None, ('blk', 'across')), may hold values from -2.4 to 2.4
- radius: float32 [262144], P(('blk', 'across')), may hold values from 0.3 to 0.6
- block_count: int32 [2048], P(('blk', 'across')), may hold values from 64 to 128, as said below
- pair_target: int32 [32, 256], P(('blk', 'across')), may hold values from 0 to 127, as said below
- pair_slot: int32 [32, 256], P(('blk', 'across')), may hold values from 0 to 319, as said below
- pair_count: int32 [32], P(('blk', 'across')), may hold values from 64 to 256, as said below
Outputs:
- velocity: float32 [3, 262144], P(None, ('blk', 'across'))
- stretching: float32 [3, 262144], P(None, ('blk', 'across'))
- section_positions: float32 [3, 262144], P(None, ('blk', 'across'))
- section_strengths: float32 [3, 262144], P(None, ('blk', 'across'))
Inputs may be any that keep to these rules, and one draw needn't show every extreme that they name: `block_count`: each block's live particles are its first slots; some block is full in every draw. Within one device's list the pairs (pair_target, pair_slot) are all different. `pair_slot`: the window's slots come in five runs of 64: slots k * 64 to (k + 1) * 64 - 1, for k = 0 to 4, are the blocks of the shard k - 2 away (two below, one below, the own shard, one above, two above, on a closed cycle of shards), each at the device's own place within its shard. `pair_count`: some shards use the whole list on every device in every draw; the others use a quarter to a half of it.
All inputs are finite; a program needn't handle non-finite values.
Results may differ from a plain program's by a relative error of at most 0.0001.
Values sent between devices are 32-bit elements; how exact they have to be, the bound alone decides.
No kernel may reach another device: no remote copies, remote signals or barrier semaphores. Data moves between devices by JAX's collectives and lax.ppermute only.
A program may use at most 64 MiB of HBM per device.

v0:
```python
import jax
import jax.numpy as jnp
from jax import lax
from jax.experimental import pallas as pl
from jax.experimental.pallas import tpu as pltpu
from jax.sharding import PartitionSpec as P

BLOCK = 128
ROWS = 8
REACH = 2
GROUP = 8
HALF = 4
FEATURES = 48
CLASSES = 8

F_SCALE = (2.0 / 3.0) ** 1.5
H_SCALE = 5.0 * (2.0 / 3.0) ** 2.5
biot_factor = 0.07957747154594767
section_step = 0.05


def moved(value, axis, target_of):
    pairs = [(source, target_of(source)) for source in range(lax.axis_size(axis))]
    return lax.ppermute(value, axis, pairs)


def to_other_core(source):
    return source ^ 1


def shifted(steps, count):
    return lambda source: (source + steps) % count


HOME_FLOPS = 10**10
NEAR_FLOPS = 10**10
FAR_FLOPS = 10**10


def rounded(value):
    return value.astype(jnp.bfloat16).astype(jnp.float32)


def split_three(value):
    first = rounded(value)
    rest = value - first
    second = rounded(rest)
    return first, second, rest - second


def six_slots(tile, order):
    parts = split_three(tile)
    return jnp.concatenate([parts[part] for part in order], axis=0).astype(jnp.bfloat16)


def cross(left, right):
    return [
        left[1] * right[2] - left[2] * right[1],
        left[2] * right[0] - left[0] * right[2],
        left[0] * right[1] - left[1] * right[0],
    ]


def tile_rows(index, rows):
    return pl.ds(pl.multiple_of(index * rows, rows), rows)


def component(ref, base, number, stride):
    return ref[pl.ds(base + number, GROUP, stride=stride), :]


def store_component(ref, base, number, stride, value):
    ref[pl.ds(base + number, GROUP, stride=stride), :] = value


def target_features(targets, step, centres, near_rows, tilt_rows):
    base = pl.multiple_of(step * (GROUP * ROWS), GROUP * ROWS)
    pos = [component(targets, base, k, ROWS) for k in range(3)]
    strength = [component(targets, base, 3 + k, ROWS) for k in range(3)]
    for k in range(3):
        centre = jnp.broadcast_to(jnp.mean(pos[k], axis=1, keepdims=True), (GROUP, BLOCK))
        store_component(centres, base, k, ROWS, centre)
        pos[k] = pos[k] - centre
    for k in range(3, ROWS):
        store_component(centres, base, k, ROWS, jnp.zeros_like(pos[0]))
    norm = pos[0] * pos[0] + pos[1] * pos[1] + pos[2] * pos[2]
    own = pos[0] * strength[0] + pos[1] * strength[1] + pos[2] * strength[2]
    near = [(2.0 / 3.0) * value for value in pos + [norm, jnp.ones_like(norm)]]
    tilt = [0.5 * s for s in strength] + [own]
    for rows, values in ((near_rows, near), (tilt_rows, tilt)):
        for k, value in enumerate(values):
            store_component(rows, 0, k, ROWS, value)


def source_features(gathered, weight, left, charge):
    pos = [component(gathered, 0, k, ROWS) for k in range(3)]
    strength = [component(gathered, 0, 3 + k, ROWS) for k in range(3)]
    inv_core = 1.0 / component(gathered, 0, 6, ROWS)
    inv_square = inv_core * inv_core
    norm = pos[0] * pos[0] + pos[1] * pos[1] + pos[2] * pos[2]
    twice = -2.0 * inv_square
    shape = [p * twice for p in pos] + [inv_square, norm * inv_square + 1.0]
    for k, value in enumerate(shape):
        store_component(left, 0, k, ROWS, value)
    scale = inv_square * inv_core * weight
    for k, value in enumerate(strength + cross(pos, strength)):
        store_component(charge, 0, k, ROWS, value * scale)


NT = (((1,), (1,)), ((), ()))
TN = (((0,), (0,)), ((), ()))


def put_tiles(window, first, tiles, length):
    base = pl.multiple_of(first * ROWS, ROWS)
    blocks = tiles.shape[0] // ROWS
    window[pl.ds(base, blocks * ROWS), :] = tiles[...]
    row = (2 * length // BLOCK + 1) * ROWS - 1
    counts = tiles[row : row + 1, :]
    row = lax.broadcasted_iota(jnp.int32, (blocks, BLOCK), 0)
    lane = lax.broadcasted_iota(jnp.int32, (blocks, BLOCK), 1)
    counts = jnp.sum(jnp.where(row == lane, counts, 0.0), axis=1, keepdims=True)
    alive = jnp.where(lane.astype(jnp.float32) < counts, 1.0, 0.0)
    for j in range(blocks // GROUP):
        part = alive[j * GROUP : (j + 1) * GROUP, :]
        for k in range(3, 6):
            rows = pl.ds(base + j * GROUP * ROWS + k, GROUP, stride=ROWS)
            window[rows, :] = window[rows, :] * part


def prepare_targets(state, near_rows, tilt_rows):
    targets, features, centres, total = state
    near_rows[...] = jnp.zeros_like(near_rows)
    tilt_rows[...] = jnp.zeros_like(tilt_rows)
    total[...] = jnp.zeros_like(total)

    def prepare(step, carry):
        target_features(targets, step, centres, near_rows, tilt_rows)
        for u in range(GROUP):
            rows = slice(u * ROWS, (u + 1) * ROWS)
            features[step * GROUP + u, :, :BLOCK] = six_slots(near_rows[rows, :], (0, 1, 2, 0, 1, 0))
            features[step * GROUP + u, :, BLOCK:] = six_slots(tilt_rows[rows, :], (0, 1, 2, 0, 1, 0))
        return carry

    lax.fori_loop(0, features.shape[0] // GROUP, prepare, 0)


def run_class(lists, window, state, scratch):
    _, features, centres, total = state
    gathered, left, charge_next, charge, first_half, second_half = scratch
    slot_row = (lists.shape[0] - 1) // 2
    listed = lists[2 * slot_row, 0]

    def entry_at(step, u):
        entry = jnp.minimum(step * GROUP + u, listed - 1)
        return entry // BLOCK, lax.rem(entry, BLOCK)

    def target_of(step, u):
        row, column = entry_at(step, u)
        return lists[row, column]

    def prepare_sources(step):
        for u in range(GROUP):
            row, column = entry_at(step, u)
            gathered[u * ROWS : (u + 1) * ROWS, :] = (
                window[tile_rows(lists[row + slot_row, column], ROWS), :]
                - centres[tile_rows(lists[row, column], ROWS), :]
            )
        order = lax.broadcasted_iota(jnp.int32, (GROUP, BLOCK), 0) + step * GROUP
        weight = jnp.where(order < listed, 1.0, 0.0).astype(jnp.float32)
        source_features(gathered, weight, left, charge_next)

    def products(step, u, held):
        shape = six_slots(left[u * ROWS : (u + 1) * ROWS, :], (0, 0, 0, 1, 1, 2))
        held[u % HALF] = lax.dot_general(
            shape, features[target_of(step, u)], TN, preferred_element_type=jnp.float32
        )

    def weights(u, held):
        near = held[u % HALF, :, :BLOCK]
        tilt = held[u % HALF, :, BLOCK:]
        q = lax.rsqrt(near)
        q2 = q * q
        q3 = q2 * q
        q5 = q3 * q2
        f = q3 + q5
        h = (q5 * tilt) * (q2 + 0.6)
        fh = f.astype(jnp.bfloat16)
        fl = (f - fh.astype(jnp.float32)).astype(jnp.bfloat16)
        hh = h.astype(jnp.bfloat16)
        hl = (h - hh.astype(jnp.float32)).astype(jnp.bfloat16)
        return jnp.concatenate(
            [jnp.concatenate([fh, fl], axis=1), jnp.concatenate([hh, hl], axis=1)], axis=0
        )

    def add_up(u, stacked):
        pair = charge[u * ROWS : (u + 1) * ROWS, :]
        high = rounded(pair)
        pair = jnp.concatenate([high, pair - high], axis=0).astype(jnp.bfloat16)
        blank = jnp.zeros_like(pair)
        pair = jnp.concatenate(
            [jnp.concatenate([pair, blank], axis=1), jnp.concatenate([blank, pair], axis=1)], axis=0
        )
        sums = jnp.dot(pair, stacked, preferred_element_type=jnp.float32)
        fsum = sums[0:8, :BLOCK] + sums[8:16, :BLOCK] + sums[0:8, BLOCK:]
        hsum = sums[16:24, :BLOCK] + sums[24:32, :BLOCK] + sums[16:24, BLOCK:]
        return jnp.concatenate([fsum, hsum], axis=0)

    def turn(step, carry):
        sums = []
        for u in range(HALF):
            stacked = weights(u, first_half)
            products(step, HALF + u, second_half)
            sums.append(add_up(u, stacked))
        prepare_sources(step + 1)
        for u in range(HALF, GROUP):
            stacked = weights(u, second_half)
            products(step + 1, u - HALF, first_half)
            sums.append(add_up(u, stacked))
        charge[...] = charge_next[...]
        for u in range(GROUP):
            total[tile_rows(target_of(step, u), 2 * ROWS), :] += sums[u]
        return carry

    @pl.when(listed > 0)
    def _():
        left[...] = jnp.zeros_like(left)
        charge_next[...] = jnp.zeros_like(charge_next)
        prepare_sources(0)
        for u in range(HALF):
            products(0, u, first_half)
        charge[...] = charge_next[...]
        lax.fori_loop(0, (listed + GROUP - 1) // GROUP, turn, 0)


def finish(targets, centres, totals, out_ref):
    blocks = out_ref.shape[1] // 6

    def one(step, carry):
        base = pl.multiple_of(step * GROUP * ROWS, GROUP * ROWS)
        wide = pl.multiple_of(step * GROUP * 2 * ROWS, GROUP * 2 * ROWS)
        pos = [
            component(targets, base, k, ROWS) - component(centres, base, k, ROWS) for k in range(3)
        ]
        strength = [component(targets, base, 3 + k, ROWS) for k in range(3)]
        fa, fb, ha, hb = [
            [
                sum(component(total, wide, start + k, 2 * ROWS) for total in totals)
                for k in range(3)
            ]
            for start in (0, 3, 8, 11)
        ]
        swirl = cross(pos, fa)
        lean = cross(strength, fa)
        bend = cross(pos, ha)
        member = step * GROUP // blocks
        inside = lax.rem(step * GROUP, blocks)
        for k in range(3):
            velocity = (-F_SCALE * biot_factor) * (swirl[k] - fb[k])
            stretch = (-F_SCALE * biot_factor) * lean[k] + (H_SCALE * biot_factor) * (bend[k] - hb[k])
            out_ref[member, pl.ds(pl.multiple_of(k * blocks + inside, GROUP), GROUP), :] = velocity
            out_ref[member, pl.ds(pl.multiple_of((3 + k) * blocks + inside, GROUP), GROUP), :] = stretch
        return carry

    lax.fori_loop(0, targets.shape[0] // ROWS // GROUP, one, 0, unroll=2)


def sort_list(number, own, length, sorted_list, blocks, members):
    rows = [own[b * ROWS + ROWS - 1 : (b + 1) * ROWS, :] for b in range(2 * length // BLOCK)]
    half = length // BLOCK
    t = jnp.concatenate(rows[:half], axis=1).astype(jnp.int32)
    s = jnp.concatenate(rows[half : 2 * half], axis=1).astype(jnp.int32)
    entry = lax.broadcasted_iota(jnp.int32, (1, length), 1)
    t = t - lax.axis_index("across") * blocks
    t = jnp.where(t < 0, t + members * blocks, t)
    run = s // blocks
    mine = t < blocks
    t = jnp.where(mine, t, t - blocks)
    near = (run == REACH) | (run == side_of_partner())
    kind = jnp.where(
        mine,
        jnp.where(near, 0, 4),
        jnp.where(near | (run == 0), 1, jnp.where(run == 2 * REACH, 2, 3)),
    )
    kind = jnp.where(entry < number, kind, CLASSES - 1)
    member = jnp.where(lax.broadcasted_iota(jnp.int32, (CLASSES, length), 0) == kind, 1.0, 0.0)
    row = lax.broadcasted_iota(jnp.int32, (length, length), 0)
    column = lax.broadcasted_iota(jnp.int32, (length, length), 1)
    before = jnp.where(row < column, 1.0, 0.0).astype(jnp.bfloat16)
    earlier = jnp.dot(member.astype(jnp.bfloat16), before, preferred_element_type=jnp.float32)
    rank = jnp.sum(member * earlier, axis=0, keepdims=True).astype(jnp.int32)
    place = jnp.where(row == rank, 1.0, 0.0).astype(jnp.bfloat16)
    values = [t // BLOCK, t % BLOCK, s // BLOCK, s % BLOCK]
    values = [member * value.astype(jnp.float32) for value in values]
    values = jnp.concatenate(values, axis=0).astype(jnp.bfloat16)
    found = lax.dot_general(values, place, NT, preferred_element_type=jnp.float32)
    number = jnp.broadcast_to(jnp.sum(member, axis=1, keepdims=True), (CLASSES, BLOCK))
    targets = found[0:8] * BLOCK + found[8:16]
    slots = found[16:24] * BLOCK + found[24:32]
    columns = [slice(j * BLOCK, (j + 1) * BLOCK) for j in range(length // BLOCK)]
    rows = sorted_list.shape[1]
    for kind in range(CLASSES - 1):
        one = slice(kind, kind + 1)
        parts = [targets[one, c] for c in columns] + [slots[one, c] for c in columns] + [number[one]]
        padding = rows - len(parts)
        if padding:
            parts.append(jnp.zeros((padding, BLOCK), jnp.float32))
        sorted_list[kind] = jnp.concatenate(parts, axis=0).astype(jnp.int32)


def list_rows(length):
    return 2 * (length // BLOCK) + 1


def read_list(kind, sorted_list, lists, sems):
    copy = pltpu.make_async_copy(sorted_list.at[kind, pl.ds(0, lists.shape[0])], lists, sems.at[0])
    copy.start()
    return copy


class shifted_window:
    def __init__(self, ref, start):
        self.ref, self.start = ref, start * ROWS

    def __getitem__(self, index):
        rows, lanes = index
        return self.ref[pl.ds(pl.multiple_of(rows.start - self.start, ROWS), rows.size), lanes]


def side_of_partner():
    return jnp.where(lax.axis_index("blk") % 2 == 0, REACH + 1, REACH - 1)


def home_kernel(number, own, partner, *refs, members, length):
    sorted_list, live, features, centres, total = refs[:5]
    window, near_rows, tilt_rows, lists, sems = refs[5:10]
    scratch = refs[10:]
    state = (live, features, centres, total)
    blocks = own.shape[0] // ROWS
    sort_list(number[0], own, length, sorted_list, blocks, members)
    to_scalars = read_list(0, sorted_list, lists, sems)
    put_tiles(live, 0, own, length)
    window[pl.ds(REACH * blocks * ROWS, blocks * ROWS), :] = live[...]
    put_tiles(window, side_of_partner() * blocks, partner, length)
    prepare_targets(state, near_rows, tilt_rows)
    to_scalars.wait()
    run_class(lists, window, state, scratch)


def near_kernel(sorted_list, live, partner, below, *refs, members, length):
    others, refs = refs[: members - 1], refs[members - 1 :]
    targets, features, centres, total = state = refs[:4]
    window, near_rows, tilt_rows, lists, sems = refs[4:9]
    scratch = refs[9:]
    to_scalars = read_list(1, sorted_list, lists, sems)
    blocks = live.shape[0] // ROWS
    window[pl.ds(REACH * blocks * ROWS, blocks * ROWS), :] = live[...]
    put_tiles(window, side_of_partner() * blocks, partner, length)
    put_tiles(window, 0, below, length)
    for r, other in enumerate(others):
        put_tiles(targets, r * blocks, other, length)
    prepare_targets(state, near_rows, tilt_rows)
    to_scalars.wait()
    run_class(lists, window, state, scratch)


def single_kernel(sorted_list, tiles, targets, features, centres, *refs, kind, run, length):
    total, window, lists, sems = refs[:4]
    to_scalars = read_list(kind, sorted_list, lists, sems)
    total[...] = jnp.zeros_like(total)
    put_tiles(window, 0, tiles, length)
    to_scalars.wait()
    window = shifted_window(window, run * (tiles.shape[0] // ROWS))
    run_class(lists, window, (targets, features, centres, total), refs[4:])


def far_kernel(sorted_list, below, above, crossed, *refs, length):
    targets, features, centres, near_total, middle_total = refs[:5]
    window, out_ref, total, lists, sems = refs[5:10]
    scratch = refs[10:]
    state = (targets, features, centres, total)
    to_scalars = read_list(3, sorted_list, lists, sems)
    blocks = below.shape[0] // ROWS
    put_tiles(window, 0, below, length)
    put_tiles(window, 2 * REACH * blocks, above, length)
    put_tiles(window, (2 * REACH - side_of_partner()) * blocks, crossed, length)
    total[...] = jnp.zeros_like(total)
    to_scalars.wait()
    run_class(lists, window, state, scratch)
    finish(targets, centres, (near_total, middle_total, total), out_ref)


def last_kernel(sorted_list, window, own, features, centres, *refs):
    home_total, out_ref, total, lists, sems = refs[:5]
    to_scalars = read_list(4, sorted_list, lists, sems)
    total[...] = jnp.zeros_like(total)
    to_scalars.wait()
    run_class(lists, window, (own, features, centres, total), refs[5:])
    finish(own, centres, (home_total, total), out_ref)


def section_kernel(own, sums, *refs):
    returned, (velocity, stretching, section_positions, section_strengths) = refs[:-4], refs[-4:]
    blocks = own.shape[0] // ROWS
    for b in range(blocks):
        lanes = slice(b * BLOCK, (b + 1) * BLOCK)
        for start, result, stepped in ((0, velocity, section_positions), (3, stretching, section_strengths)):
            chosen = pl.ds(start * blocks + b, 3, stride=blocks)
            value = sums[chosen, :]
            for other in returned:
                value = value + other[chosen, :]
            result[:, lanes] = value
            first = b * ROWS + start
            stepped[:, lanes] = own[first : first + 3, :] + section_step * value


def call(kernel, name, inputs, outputs, scratch, flops=0):
    vmem = pl.BlockSpec(memory_space=pltpu.VMEM)
    smem = pl.BlockSpec(memory_space=pltpu.SMEM)
    held = sum(value.size * value.dtype.itemsize for value in (*inputs, *outputs))
    return pl.pallas_call(
        kernel,
        out_shape=outputs,
        in_specs=[smem if value.dtype == jnp.int32 and value.ndim == 1 else vmem for value in inputs],
        out_specs=[vmem for value in outputs],
        scratch_shapes=scratch,
        compiler_params=pltpu.CompilerParams(vmem_limit_bytes=10 * 1024 * 1024 + 2 * held),
        cost_estimate=pl.CostEstimate(flops=flops, bytes_accessed=0, transcendentals=0),
        name=name,
    )(*inputs)


def shards(positions, strengths, radius, block_count, pair_target, pair_slot, pair_count):
    blocks = block_count.shape[0]
    lanes = blocks * BLOCK
    length = pair_target.shape[1]
    members = lax.axis_size("across")
    shard = lax.axis_index("blk")
    count = lax.axis_size("blk")

    def f32(*shape):
        return jax.ShapeDtypeStruct(shape, jnp.float32)

    parts = [value.reshape(3, blocks, BLOCK).transpose(1, 0, 2) for value in (positions, strengths)]
    rows, start = [], 0
    for value in (pair_target[0], pair_slot[0], block_count):
        rows.append(jnp.pad(value, (start, lanes - start - value.shape[0])))
        start += -(-value.shape[0] // BLOCK) * BLOCK
    listed = sum(rows).astype(jnp.float32).reshape(blocks, 1, BLOCK)
    own = jnp.concatenate(parts + [radius.reshape(blocks, 1, BLOCK), listed], axis=1)
    own = own.reshape(blocks * ROWS, BLOCK)
    others = [
        moved(own, "across", lambda source: (source - away) % members) for away in range(1, members)
    ]
    partner = moved(own, "blk", to_other_core)
    below = moved(own, "blk", shifted(REACH, count))

    def state_shapes(number):
        return [
            f32(number * blocks * ROWS, BLOCK),
            jax.ShapeDtypeStruct((number * blocks, FEATURES, 2 * BLOCK), jnp.bfloat16),
            f32(number * blocks * ROWS, BLOCK),
            f32(number * blocks * 2 * ROWS, BLOCK),
        ]

    own_shapes, other_shapes = state_shapes(1), state_shapes(members - 1)
    window_shape = f32((2 * REACH + 1) * blocks * ROWS, BLOCK)
    rows = list_rows(length)
    list_shape = jax.ShapeDtypeStruct((CLASSES - 1, -(-rows // ROWS) * ROWS, BLOCK), jnp.int32)
    feature_rows = [pltpu.VMEM((GROUP * ROWS, BLOCK), jnp.float32)] * 2
    list_scratch = [pltpu.SMEM((rows, BLOCK), jnp.int32), pltpu.SemaphoreType.DMA((1,))]
    scratch = [pltpu.VMEM((GROUP * ROWS, BLOCK), jnp.float32)] * 4 + [
        pltpu.VMEM((HALF, BLOCK, 2 * BLOCK), jnp.float32),
        pltpu.VMEM((HALF, BLOCK, 2 * BLOCK), jnp.float32),
    ]
    window_scratch = pltpu.VMEM(window_shape.shape, jnp.float32)

    lists, live, *own_state = call(
        lambda *refs: home_kernel(*refs, members=members, length=length),
        "home_pairs",
        (pair_count, own, partner),
        [list_shape] + own_shapes,
        [window_scratch] + feature_rows + list_scratch + scratch,
        flops=HOME_FLOPS,
    )
    late, lists = lax.optimization_barrier((own, lists))
    above = moved(late, "blk", shifted(-REACH, count))
    other_state = list(call(
        lambda *refs: near_kernel(*refs, members=members, length=length),
        "near_pairs",
        (lists, live, partner, below, *others),
        other_shapes,
        [window_scratch] + feature_rows + list_scratch + scratch,
        flops=NEAR_FLOPS,
    ))
    above, other_state[3] = lax.optimization_barrier((above, other_state[3]))
    crossed = moved(jnp.where(shard % 2 == 0, above, below), "blk", to_other_core)
    (middle_total,) = call(
        lambda *refs: single_kernel(*refs, kind=2, run=2 * REACH, length=length),
        "middle_pairs",
        (lists, above, *other_state[:3]),
        [other_shapes[3]],
        [pltpu.VMEM(own.shape, jnp.float32)] + list_scratch + scratch,
        flops=HOME_FLOPS,
    )
    crossed, middle_total = lax.optimization_barrier((crossed, middle_total))
    window, away_sums = call(
        lambda *refs: far_kernel(*refs, length=length),
        "far_pairs",
        (lists, below, above, crossed, *other_state, middle_total),
        [window_shape, f32(members - 1, 6 * blocks, BLOCK)],
        [pltpu.VMEM(other_shapes[3].shape, jnp.float32)] + list_scratch + scratch,
        flops=FAR_FLOPS,
    )
    returned = [
        moved(away_sums[away - 1], "across", lambda source: (source + away) % members)
        for away in range(1, members)
    ]
    (sums,) = call(
        last_kernel,
        "last_pairs",
        (lists, window, live, *own_state),
        [f32(1, 6 * blocks, BLOCK)],
        [pltpu.VMEM(own_shapes[3].shape, jnp.float32)] + list_scratch + scratch,
        flops=FAR_FLOPS,
    )
    wide = f32(3, lanes)
    return tuple(
        call(section_kernel, "section", (live, sums[0], *returned), [wide] * 4, [])
    )


def solution(mesh):
    whole = P(None, ("blk", "across"))
    line = P(("blk", "across"))
    return jax.shard_map(
        shards,
        mesh=mesh,
        in_specs=(whole, whole, line, line, P(("blk", "across"), None), P(("blk", "across"), None), line),
        out_specs=(whole, whole, whole, whole),
        check_vma=False,
    )
```

profile of v0, /device:TPU:0, one launch (start us, length us, event | category | flops | bytes accessed | tf_op | source)
XLA Modules:
  0.0 37.8 jit_solution(2206844211484019542)
XLA Ops:
  0.6 0.7 %add_convert_fusion = f32[8192]{0:T(1024)S(1)} fusion(s32[64]{0:T(128)} %param.10, s32[256]{0:T(256)} %bitcast.20, s32[256]{0:T(256)} %bitcast.21), kind=kLoop, calls=%fused_computation.2 | loop fusion | flops 24576 | bytes 35072 | tf_op jit(solution)/shard_map/convert_element_type | solution.py:449
  1.4 1.1 %maximum_bitcast_fusion.refs_1_ = f32[512,128]{1,0:T(8,128)S(1)} fusion(f32[64,1,128]{2,1,0:T(1,128)S(1)} %bitcast.16, f32[64,1,128]{2,1,0:T(1,128)} %bitcast.19, f32[64,3,128]{2,1,0:T(4,128)} %bitcast.17, f32[64,3,128]{2,1,0:T(4,128)} %bitcast.18), kind=kLoop, calls=%fused_computation | loop fusion | flops 196608 | bytes 524288 | tf_op jit(solution)/shard_map/reshape | solution.py:451
  2.5 0.5 %collective-permute-start = (f32[512,128]{1,0:T(8,128)S(1)}, f32[512,128]{1,0:T(8,128)S(1)}, u32[]{:S(2)}, u32[]{:S(2)}) collective-permute-start(f32[512,128]{1,0:T(8,128)S(1)} %maximum_bitcast_fusion.refs_1_), channel_id=1, source_target_pairs={{0,2},{2,0},{4,6},{6,4},{8,10},{10,8},{12,14},{14,12},{16,18},{18,... | collective-permute-start | bytes 786440 | tf_op jit(solution)/shard_map/ppermute | solution.py:24
  3.0 2.6 %collective-permute-start.3 = (f32[512,128]{1,0:T(8,128)S(1)}, f32[512,128]{1,0:T(8,128)S(1)}, u32[]{:S(2)}, u32[]{:S(2)}) collective-permute-start(f32[512,128]{1,0:T(8,128)S(1)} %maximum_bitcast_fusion.refs_1_), channel_id=1, source_target_pairs={{0,1},{1,0},{2,3},{3,2},{4,5},{5,4},{6,7},{7,6},{8,9},{9,8},{10,11... | collective-permute-start | bytes 786440 | tf_op jit(solution)/shard_map/ppermute | solution.py:24
  5.5 1.5 %collective-permute-start.1 = (f32[512,128]{1,0:T(8,128)S(1)}, f32[512,128]{1,0:T(8,128)S(1)}, u32[]{:S(2)}, u32[]{:S(2)}) collective-permute-start(f32[512,128]{1,0:T(8,128)S(1)} %maximum_bitcast_fusion.refs_1_), channel_id=1, source_target_pairs={{0,4},{2,6},{4,8},{6,10},{8,12},{10,14},{12,16},{14,18},{16,20},{1... | collective-permute-start | bytes 786440 | tf_op jit(solution)/shard_map/ppermute | solution.py:24
  7.7 0.0 collective-permute-done.refs_2_
  7.7 5.3 %home_pairs.1 = (s32[7,8,128]{2,1,0:T(8,128)S(1)}, f32[512,128]{1,0:T(8,128)S(1)}, bf16[64,48,256]{2,1,0:T(8,128)(2,1)S(1)}, f32[512,128]{1,0:T(8,128)S(1)}, f32[1024,128]{1,0:T(8,128)S(1)}) custom-call(s32[1]{0:T(128)S(6)} %copy.13.refs_0_, f32[512,128]{1,0:T(8,128)S(1)} %maximum_bitcast_fusion.refs_1_, f32[512,128]{1,0:T(8,128)S(1)} %collective-permute-done.refs_2_), custom_call_target="tpu_custom_call" | custom-call | flops 10000000000 | tf_op jit(solution)/shard_map/home_pairs/pallas_call | solution.py:421
  13.1 1.2 %collective-permute-start.2 = (f32[512,128]{1,0:T(8,128)S(1)}, f32[512,128]{1,0:T(8,128)S(1)}, u32[]{:S(2)}, u32[]{:S(2)}) collective-permute-start(f32[512,128]{1,0:T(8,128)S(1)} %maximum_bitcast_fusion.refs_1_), channel_id=1, source_target_pairs={{0,28},{2,30},{4,0},{6,2},{8,4},{10,6},{12,8},{14,10},{16,12},{18,... | collective-permute-start | bytes 786440 | tf_op jit(solution)/shard_map/ppermute | solution.py:24
  14.3 0.0 collective-permute-done.3.refs_4_
  14.3 2.6 %collective-permute-done.1.refs_3_.refs_1_ = f32[512,128]{1,0:T(8,128)S(1)} collective-permute-done((f32[512,128]{1,0:T(8,128)S(1)}, f32[512,128]{1,0:T(8,128)S(1)}, u32[]{:S(2)}, u32[]{:S(2)}) %collective-permute-start.1) | collective-permute-done | bytes 262176 | tf_op jit(solution)/shard_map/ppermute | solution.py:24
  16.8 6.7 %near_pairs.1 = (f32[512,128]{1,0:T(8,128)S(1)}, bf16[64,48,256]{2,1,0:T(8,128)(2,1)S(1)}, f32[512,128]{1,0:T(8,128)S(1)}, f32[1024,128]{1,0:T(8,128)S(1)}) custom-call(s32[7,8,128]{2,1,0:T(8,128)S(1)} %get-tuple-element.23.refs_0_.sorted_list, f32[512,128]{1,0:T(8,128)S(1)} %get-tuple-element.21.refs_1_.own, f32[512,128]{1,0:T(8,128)S(1)} %collective-permute-done.refs_2_, ...), custom_call_target="tpu_custom_call" | custom-call | flops 10000000000 | tf_op jit(solution)/shard_map/near_pairs/pallas_call | solution.py:421
  23.6 0.0 collective-permute-done.2.refs_1_.refs_2_
  23.6 0.1 collective-permute-start.4
  23.7 2.5 %middle_pairs.1.refs_8_ = f32[1024,128]{1,0:T(8,128)S(1)} custom-call(s32[7,8,128]{2,1,0:T(8,128)S(1)} %get-tuple-element.23.refs_0_.sorted_list, f32[512,128]{1,0:T(8,128)S(1)} %collective-permute-done.2.refs_1_.refs_2_, f32[512,128]{1,0:T(8,128)S(1)} %get-tuple-element.27.refs_2_.refs_4_, bf16[64,48,256]{2,1,0:T(8,128)(2,1)S(1)} %get-tuple-element.28.refs_3_.refs_5_, ...), custom_call_target="tpu_custom_call" | custom-call | flops 10000000000 | tf_op jit(solution)/shard_map/middle_pairs/pallas_call | solution.py:421
  26.2 0.0 collective-permute-done.4.refs_3_
  26.2 3.4 %far_pairs.1 = (f32[2560,128]{1,0:T(8,128)S(1)}, f32[1,384,128]{2,1,0:T(8,128)S(1)}) custom-call(s32[7,8,128]{2,1,0:T(8,128)S(1)} %get-tuple-element.23.refs_0_.sorted_list, f32[512,128]{1,0:T(8,128)S(1)} %collective-permute-done.1.refs_3_.refs_1_, f32[512,128]{1,0:T(8,128)S(1)} %collective-permute-done.2.refs_1_.refs_2_, ...), custom_call_target="tpu_custom_call" | custom-call | flops 10000000000 | tf_op jit(solution)/shard_map/far_pairs/pallas_call | solution.py:421
  29.6 1.1 %collective-permute-start.5 = (f32[384,128]{1,0:T(8,128)S(1)}, f32[384,128]{1,0:T(8,128)S(1)}, u32[]{:S(2)}, u32[]{:S(2)}) collective-permute-start(f32[384,128]{1,0:T(8,128)S(1)} %bitcast.15), channel_id=1, source_target_pairs={{0,1},{1,0},{2,3},{3,2},{4,5},{5,4},{6,7},{7,6},{8,9},{9,8},{10,11... | collective-permute-start | bytes 589832 | tf_op jit(solution)/shard_map/ppermute | solution.py:24
  30.7 5.9 %last_pairs.1 = f32[1,384,128]{2,1,0:T(8,128)S(1)} custom-call(s32[7,8,128]{2,1,0:T(8,128)S(1)} %get-tuple-element.23.refs_0_.sorted_list, f32[2560,128]{1,0:T(8,128)S(1)} %get-tuple-element.33.window, f32[512,128]{1,0:T(8,128)S(1)} %get-tuple-element.21.refs_1_.own, bf16[64,48,256]{2,1,0:T(8,128)(2,1)S(1)} %get-tuple-element.34.features, ...), custom_call_target="tpu_custom_call" | custom-call | flops 10000000000 | tf_op jit(solution)/shard_map/last_pairs/pallas_call | solution.py:421
  36.6 0.0 collective-permute-done.5.refs_0_
  36.7 1.1 %section.1 = (f32[3,8192]{1,0:T(4,128)}, f32[3,8192]{1,0:T(4,128)}, f32[3,8192]{1,0:T(4,128)}, f32[3,8192]{1,0:T(4,128)}) custom-call(f32[512,128]{1,0:T(8,128)S(1)} %get-tuple-element.21.refs_1_.own, f32[384,128]{1,0:T(8,128)S(1)} %bitcast.14, f32[384,128]{1,0:T(8,128)S(1)} %collective-permute-done.5.refs_0_), custom_call_target="tpu_custom_call" | custom-call | tf_op jit(solution)/shard_map/section/pallas_call | solution.py:421
  (1 shorter events, 0.0 us)
Async XLA Ops:
  2.5 5.3 %collective-permute-start = (f32[512,128]{1,0:T(8,128)S(1)}, f32[512,128]{1,0:T(8,128)S(1)}, u32[]{:S(2)}, u32[]{:S(2)}) collective-permute-start(f32[512,128]{1,0:T(8,128)S(1)} %maximum_bitcast_fusion.refs_1_), channel_id=1, source_target_pairs={{0,2},{2,0},{4,6},{6,4},{8,10},{10,8},{12,14},{14,12},{16,18},{18,... | collective-permute-start | bytes 786440 | tf_op jit(solution)/shard_map/ppermute | solution.py:24
  3.0 11.3 %collective-permute-start.3 = (f32[512,128]{1,0:T(8,128)S(1)}, f32[512,128]{1,0:T(8,128)S(1)}, u32[]{:S(2)}, u32[]{:S(2)}) collective-permute-start(f32[512,128]{1,0:T(8,128)S(1)} %maximum_bitcast_fusion.refs_1_), channel_id=1, source_target_pairs={{0,1},{1,0},{2,3},{3,2},{4,5},{5,4},{6,7},{7,6},{8,9},{9,8},{10,11... | collective-permute-start | bytes 786440 | tf_op jit(solution)/shard_map/ppermute | solution.py:24
  5.5 11.3 %collective-permute-start.1 = (f32[512,128]{1,0:T(8,128)S(1)}, f32[512,128]{1,0:T(8,128)S(1)}, u32[]{:S(2)}, u32[]{:S(2)}) collective-permute-start(f32[512,128]{1,0:T(8,128)S(1)} %maximum_bitcast_fusion.refs_1_), channel_id=1, source_target_pairs={{0,4},{2,6},{4,8},{6,10},{8,12},{10,14},{12,16},{14,18},{16,20},{1... | collective-permute-start | bytes 786440 | tf_op jit(solution)/shard_map/ppermute | solution.py:24
  13.1 10.5 %collective-permute-start.2 = (f32[512,128]{1,0:T(8,128)S(1)}, f32[512,128]{1,0:T(8,128)S(1)}, u32[]{:S(2)}, u32[]{:S(2)}) collective-permute-start(f32[512,128]{1,0:T(8,128)S(1)} %maximum_bitcast_fusion.refs_1_), channel_id=1, source_target_pairs={{0,28},{2,30},{4,0},{6,2},{8,4},{10,6},{12,8},{14,10},{16,12},{18,... | collective-permute-start | bytes 786440 | tf_op jit(solution)/shard_map/ppermute | solution.py:24
  23.6 2.6 %collective-permute-start.4 = (f32[512,128]{1,0:T(8,128)S(1)}, f32[512,128]{1,0:T(8,128)S(1)}, u32[]{:S(2)}, u32[]{:S(2)}) collective-permute-start(f32[512,128]{1,0:T(8,128)S(1)} %broadcast_select_fusion), channel_id=1, source_target_pairs={{0,2},{2,0},{4,6},{6,4},{8,10},{10,8},{12,14},{14,12},{16,18},{18,... | collective-permute-start | bytes 786440 | tf_op jit(solution)/shard_map/ppermute | solution.py:24
  29.6 7.0 %collective-permute-start.5 = (f32[384,128]{1,0:T(8,128)S(1)}, f32[384,128]{1,0:T(8,128)S(1)}, u32[]{:S(2)}, u32[]{:S(2)}) collective-permute-start(f32[384,128]{1,0:T(8,128)S(1)} %bitcast.15), channel_id=1, source_target_pairs={{0,1},{1,0},{2,3},{3,2},{4,5},{5,4},{6,7},{7,6},{8,9},{9,8},{10,11... | collective-permute-start | bytes 589832 | tf_op jit(solution)/shard_map/ppermute | solution.py:24
where the time goes:
time: 38 us; the launch traced here: 37.8 us
  Pallas kernels  25 us (66%)
  starting transfers between devices  6.96 us (18%)
  waiting for transfers between devices  2.6 us (7%)
  other arithmetic  1.86 us (5%)
  between operations  1.38 us (4%)
    pallas_call x6, Pallas kernels, call(): pl.pallas_call(kernel, out_shape=outputs, in_specs=[smem if value.dtype =...  25 us
    ppermute x6, starting transfers between devices, moved(): return lax.ppermute(value, axis, pairs)  6.96 us
    ppermute x6, waiting for transfers between devices, moved(): return lax.ppermute(value, axis, pairs)  2.6 us
    reshape x1, other arithmetic, shards(): own = own.reshape(blocks * ROWS, BLOCK)  1.11 us
  transfers between devices with their start and end apart: 6, of which 1 were waited for; matrix products, arithmetic and copies ran while one was open for 0% of the time, Pallas kernels for 54%

commit v1 on v0

--- a/solution.py
+++ b/solution.py
@@ -230,7 +230,14 @@
         for u in range(HALF):
             products(0, u, first_half)
         charge[...] = charge_next[...]
-        lax.fori_loop(0, (listed + GROUP - 1) // GROUP, turn, 0)
+        full = (listed + HALF - 1) // GROUP
+        lax.fori_loop(0, full, turn, 0)
+
+        @pl.when(listed > full * GROUP)
+        def _():
+            sums = [add_up(u, weights(u, first_half)) for u in range(HALF)]
+            for u in range(HALF):
+                total[tile_rows(target_of(full, u), 2 * ROWS), :] += sums[u]
 
 
 def finish(targets, centres, totals, out_ref):
@@ -279,7 +286,7 @@
     near = (run == REACH) | (run == side_of_partner())
     kind = jnp.where(
         mine,
-        jnp.where(near, 0, 4),
+        jnp.where(near, 0, jnp.where(run == 0, 5, 4)),
         jnp.where(near | (run == 0), 1, jnp.where(run == 2 * REACH, 2, 3)),
     )
     kind = jnp.where(entry < number, kind, CLASSES - 1)
@@ -349,11 +356,14 @@
 
 def near_kernel(sorted_list, live, partner, below, *refs, members, length):
     others, refs = refs[: members - 1], refs[members - 1 :]
-    targets, features, centres, total = state = refs[:4]
-    window, near_rows, tilt_rows, lists, sems = refs[4:9]
-    scratch = refs[9:]
+    own_features, own_centres = refs[:2]
+    targets, features, centres, total = state = refs[2:6]
+    own_total, window, near_rows, tilt_rows, own_lists, own_sems, lists, sems = refs[6:14]
+    scratch = refs[14:]
     to_scalars = read_list(1, sorted_list, lists, sems)
+    own_to_scalars = read_list(5, sorted_list, own_lists, own_sems)
     blocks = live.shape[0] // ROWS
+    own_total[...] = jnp.zeros_like(own_total)
     window[pl.ds(REACH * blocks * ROWS, blocks * ROWS), :] = live[...]
     put_tiles(window, side_of_partner() * blocks, partner, length)
     put_tiles(window, 0, below, length)
@@ -362,6 +372,8 @@
     prepare_targets(state, near_rows, tilt_rows)
     to_scalars.wait()
     run_class(lists, window, state, scratch)
+    own_to_scalars.wait()
+    run_class(own_lists, window, (live, own_features, own_centres, own_total), scratch)
 
 
 def single_kernel(sorted_list, tiles, targets, features, centres, *refs, kind, run, length):
@@ -391,12 +403,12 @@
 
 
 def last_kernel(sorted_list, window, own, features, centres, *refs):
-    home_total, out_ref, total, lists, sems = refs[:5]
+    home_total, near_total, out_ref, total, lists, sems = refs[:6]
     to_scalars = read_list(4, sorted_list, lists, sems)
     total[...] = jnp.zeros_like(total)
     to_scalars.wait()
-    run_class(lists, window, (own, features, centres, total), refs[5:])
-    finish(own, centres, (home_total, total), out_ref)
+    run_class(lists, window, (own, features, centres, total), refs[6:])
+    finish(own, centres, (home_total, near_total, total), out_ref)
 
 
 def section_kernel(own, sums, *refs):
@@ -485,12 +497,12 @@
     )
     late, lists = lax.optimization_barrier((own, lists))
     above = moved(late, "blk", shifted(-REACH, count))
-    other_state = list(call(
+    *other_state, near_own_total = list(call(
         lambda *refs: near_kernel(*refs, members=members, length=length),
         "near_pairs",
-        (lists, live, partner, below, *others),
-        other_shapes,
-        [window_scratch] + feature_rows + list_scratch + scratch,
+        (lists, live, partner, below, *others, *own_state[:2]),
+        other_shapes + [own_shapes[3]],
+        [window_scratch] + feature_rows + 2 * list_scratch + scratch,
         flops=NEAR_FLOPS,
     ))
     above, other_state[3] = lax.optimization_barrier((above, other_state[3]))
@@ -519,7 +531,7 @@
     (sums,) = call(
         last_kernel,
         "last_pairs",
-        (lists, window, live, *own_state),
+        (lists, window, live, *own_state, near_own_total),
         [f32(1, 6 * blocks, BLOCK)],
         [pltpu.VMEM(own_shapes[3].shape, jnp.float32)] + list_scratch + scratch,
         flops=FAR_FLOPS,

time: 38 us -> 38.9 us (1.024)
  waiting for transfers between devices: 2.6 us -> 4.06 us
  starting transfers between devices: 6.96 us -> 5.91 us
  Pallas kernels: 25 us -> 25.7 us
    ppermute x6, waiting for transfers between devices: 2.6 us -> 4.06 us  [moved(): return lax.ppermute(value, axis, pairs)]
    ppermute x6, starting transfers between devices: 6.96 us -> 5.91 us  [moved(): return lax.ppermute(value, axis, pairs)]
    pallas_call x6, Pallas kernels: 25 us -> 25.7 us  [call(): pl.pallas_call(kernel, out_shape=outputs, in_specs=[smem if value.dtype =...]
  transfers between devices with their start and end apart: 6 -> 6, of which waited for: 1 -> 2; matrix products, arithmetic and copies ran while one was open for 0% -> 0% of each run, Pallas kernels for 54% -> 54%
where the time goes in v1:
time: 38.9 us; the launch traced here: 39 us
  Pallas kernels  25.7 us (66%)
  starting transfers between devices  5.91 us (15%)
  waiting for transfers between devices  4.06 us (10%)
  other arithmetic  1.86 us (5%)
  between operations  1.37 us (4%)
    pallas_call x6, Pallas kernels, call(): pl.pallas_call(kernel, out_shape=outputs, in_specs=[smem if value.dtype =...  25.7 us
    ppermute x6, starting transfers between devices, moved(): return lax.ppermute(value, axis, pairs)  5.91 us
    ppermute x6, waiting for transfers between devices, moved(): return lax.ppermute(value, axis, pairs)  4.06 us
    reshape x1, other arithmetic, shards(): own = own.reshape(blocks * ROWS, BLOCK)  1.11 us
  transfers between devices with their start and end apart: 6, of which 2 were waited for; matrix products, arithmetic and copies ran while one was open for 0% of the time, Pallas kernels for 54%

profile of v1, /device:TPU:0, one launch (start us, length us, event | category | flops | bytes accessed | tf_op | source)
XLA Modules:
  0.0 39.0 jit_solution(11714327277157170250)
XLA Ops:
  0.6 0.7 %add_convert_fusion = f32[8192]{0:T(1024)S(1)} fusion(s32[64]{0:T(128)} %param.10, s32[256]{0:T(256)} %bitcast.20, s32[256]{0:T(256)} %bitcast.21), kind=kLoop, calls=%fused_computation.2 | loop fusion | flops 24576 | bytes 35072 | tf_op jit(solution)/shard_map/convert_element_type | solution.py:461
  1.4 1.1 %maximum_bitcast_fusion.refs_1_ = f32[512,128]{1,0:T(8,128)S(1)} fusion(f32[64,1,128]{2,1,0:T(1,128)S(1)} %bitcast.16, f32[64,1,128]{2,1,0:T(1,128)} %bitcast.19, f32[64,3,128]{2,1,0:T(4,128)} %bitcast.17, f32[64,3,128]{2,1,0:T(4,128)} %bitcast.18), kind=kLoop, calls=%fused_computation | loop fusion | flops 196608 | bytes 524288 | tf_op jit(solution)/shard_map/reshape | solution.py:463
  2.5 0.5 %collective-permute-start = (f32[512,128]{1,0:T(8,128)S(1)}, f32[512,128]{1,0:T(8,128)S(1)}, u32[]{:S(2)}, u32[]{:S(2)}) collective-permute-start(f32[512,128]{1,0:T(8,128)S(1)} %maximum_bitcast_fusion.refs_1_), channel_id=1, source_target_pairs={{0,2},{2,0},{4,6},{6,4},{8,10},{10,8},{12,14},{14,12},{16,18},{18,... | collective-permute-start | bytes 786440 | tf_op jit(solution)/shard_map/ppermute | solution.py:24
  3.0 2.6 %collective-permute-start.3 = (f32[512,128]{1,0:T(8,128)S(1)}, f32[512,128]{1,0:T(8,128)S(1)}, u32[]{:S(2)}, u32[]{:S(2)}) collective-permute-start(f32[512,128]{1,0:T(8,128)S(1)} %maximum_bitcast_fusion.refs_1_), channel_id=1, source_target_pairs={{0,1},{1,0},{2,3},{3,2},{4,5},{5,4},{6,7},{7,6},{8,9},{9,8},{10,11... | collective-permute-start | bytes 786440 | tf_op jit(solution)/shard_map/ppermute | solution.py:24
  5.5 1.5 %collective-permute-start.1 = (f32[512,128]{1,0:T(8,128)S(1)}, f32[512,128]{1,0:T(8,128)S(1)}, u32[]{:S(2)}, u32[]{:S(2)}) collective-permute-start(f32[512,128]{1,0:T(8,128)S(1)} %maximum_bitcast_fusion.refs_1_), channel_id=1, source_target_pairs={{0,4},{2,6},{4,8},{6,10},{8,12},{10,14},{12,16},{14,18},{16,20},{1... | collective-permute-start | bytes 786440 | tf_op jit(solution)/shard_map/ppermute | solution.py:24
  7.7 0.0 collective-permute-done.refs_2_
  7.7 5.3 %home_pairs.1 = (s32[7,8,128]{2,1,0:T(8,128)S(1)}, f32[512,128]{1,0:T(8,128)S(1)}, bf16[64,48,256]{2,1,0:T(8,128)(2,1)S(1)}, f32[512,128]{1,0:T(8,128)S(1)}, f32[1024,128]{1,0:T(8,128)S(1)}) custom-call(s32[1]{0:T(128)S(6)} %copy.13.refs_0_, f32[512,128]{1,0:T(8,128)S(1)} %maximum_bitcast_fusion.refs_1_, f32[512,128]{1,0:T(8,128)S(1)} %collective-permute-done.refs_2_), custom_call_target="tpu_custom_call" | custom-call | flops 10000000000 | tf_op jit(solution)/shard_map/home_pairs/pallas_call | solution.py:433
  13.1 0.7 %collective-permute-start.2 = (f32[512,128]{1,0:T(8,128)S(1)}, f32[512,128]{1,0:T(8,128)S(1)}, u32[]{:S(2)}, u32[]{:S(2)}) collective-permute-start(f32[512,128]{1,0:T(8,128)S(1)} %maximum_bitcast_fusion.refs_1_), channel_id=1, source_target_pairs={{0,28},{2,30},{4,0},{6,2},{8,4},{10,6},{12,8},{14,10},{16,12},{18,... | collective-permute-start | bytes 786440 | tf_op jit(solution)/shard_map/ppermute | solution.py:24
  13.7 0.0 collective-permute-done.3.refs_4_
  13.7 3.1 %collective-permute-done.1.refs_3_.refs_1_ = f32[512,128]{1,0:T(8,128)S(1)} collective-permute-done((f32[512,128]{1,0:T(8,128)S(1)}, f32[512,128]{1,0:T(8,128)S(1)}, u32[]{:S(2)}, u32[]{:S(2)}) %collective-permute-start.1) | collective-permute-done | bytes 262176 | tf_op jit(solution)/shard_map/ppermute | solution.py:24
  16.8 8.7 %near_pairs.1 = (f32[512,128]{1,0:T(8,128)S(1)}, bf16[64,48,256]{2,1,0:T(8,128)(2,1)S(1)}, f32[512,128]{1,0:T(8,128)S(1)}, f32[1024,128]{1,0:T(8,128)S(1)}, f32[1024,128]{1,0:T(8,128)S(1)}) custom-call(s32[7,8,128]{2,1,0:T(8,128)S(1)} %get-tuple-element.24.refs_0_.sorted_list, f32[512,128]{1,0:T(8,128)S(1)} %get-tuple-element.22.refs_1_.own, ...), custom_call_target="tpu_custom_call" | custom-call | flops 10000000000 | tf_op jit(solution)/shard_map/near_pairs/pallas_call | solution.py:433
  25.5 0.0 collective-permute-done.2.refs_1_.refs_2_
  25.6 0.1 collective-permute-start.4
  25.6 3.0 %middle_pairs.1.refs_8_ = f32[1024,128]{1,0:T(8,128)S(1)} custom-call(s32[7,8,128]{2,1,0:T(8,128)S(1)} %get-tuple-element.24.refs_0_.sorted_list, f32[512,128]{1,0:T(8,128)S(1)} %collective-permute-done.2.refs_1_.refs_2_, f32[512,128]{1,0:T(8,128)S(1)} %get-tuple-element.30.refs_2_.refs_4_, bf16[64,48,256]{2,1,0:T(8,128)(2,1)S(1)} %get-tuple-element.31.refs_3_.refs_5_, ...), custom_call_target="tpu_custom_call" | custom-call | flops 10000000000 | tf_op jit(solution)/shard_map/middle_pairs/pallas_call | solution.py:433
  28.7 0.0 collective-permute-done.4.refs_3_
  28.7 3.4 %far_pairs.1 = (f32[2560,128]{1,0:T(8,128)S(1)}, f32[1,384,128]{2,1,0:T(8,128)S(1)}) custom-call(s32[7,8,128]{2,1,0:T(8,128)S(1)} %get-tuple-element.24.refs_0_.sorted_list, f32[512,128]{1,0:T(8,128)S(1)} %collective-permute-done.1.refs_3_.refs_1_, f32[512,128]{1,0:T(8,128)S(1)} %collective-permute-done.2.refs_1_.refs_2_, ...), custom_call_target="tpu_custom_call" | custom-call | flops 10000000000 | tf_op jit(solution)/shard_map/far_pairs/pallas_call | solution.py:433
  32.1 0.6 %collective-permute-start.5 = (f32[384,128]{1,0:T(8,128)S(1)}, f32[384,128]{1,0:T(8,128)S(1)}, u32[]{:S(2)}, u32[]{:S(2)}) collective-permute-start(f32[384,128]{1,0:T(8,128)S(1)} %bitcast.15), channel_id=1, source_target_pairs={{0,1},{1,0},{2,3},{3,2},{4,5},{5,4},{6,7},{7,6},{8,9},{9,8},{10,11... | collective-permute-start | bytes 589832 | tf_op jit(solution)/shard_map/ppermute | solution.py:24
  32.7 4.2 %last_pairs.1 = f32[1,384,128]{2,1,0:T(8,128)S(1)} custom-call(s32[7,8,128]{2,1,0:T(8,128)S(1)} %get-tuple-element.24.refs_0_.sorted_list, f32[2560,128]{1,0:T(8,128)S(1)} %get-tuple-element.36.window, f32[512,128]{1,0:T(8,128)S(1)} %get-tuple-element.22.refs_1_.own, bf16[64,48,256]{2,1,0:T(8,128)(2,1)S(1)} %get-tuple-element.26.refs_5_.features, ...), custom_call_target="tpu_custom_call" | custom-call | flops 10000000000 | tf_op jit(solution)/shard_map/last_pairs/pallas_call | solution.py:433
  36.9 1.0 %collective-permute-done.5.refs_0_ = f32[384,128]{1,0:T(8,128)S(1)} collective-permute-done((f32[384,128]{1,0:T(8,128)S(1)}, f32[384,128]{1,0:T(8,128)S(1)}, u32[]{:S(2)}, u32[]{:S(2)}) %collective-permute-start.5) | collective-permute-done | bytes 196640 | tf_op jit(solution)/shard_map/ppermute | solution.py:24
  37.8 1.1 %section.1 = (f32[3,8192]{1,0:T(4,128)}, f32[3,8192]{1,0:T(4,128)}, f32[3,8192]{1,0:T(4,128)}, f32[3,8192]{1,0:T(4,128)}) custom-call(f32[512,128]{1,0:T(8,128)S(1)} %get-tuple-element.22.refs_1_.own, f32[384,128]{1,0:T(8,128)S(1)} %bitcast.14, f32[384,128]{1,0:T(8,128)S(1)} %collective-permute-done.5.refs_0_), custom_call_target="tpu_custom_call" | custom-call | tf_op jit(solution)/shard_map/section/pallas_call | solution.py:433
  (1 shorter events, 0.0 us)
Async XLA Ops:
  2.5 5.3 %collective-permute-start = (f32[512,128]{1,0:T(8,128)S(1)}, f32[512,128]{1,0:T(8,128)S(1)}, u32[]{:S(2)}, u32[]{:S(2)}) collective-permute-start(f32[512,128]{1,0:T(8,128)S(1)} %maximum_bitcast_fusion.refs_1_), channel_id=1, source_target_pairs={{0,2},{2,0},{4,6},{6,4},{8,10},{10,8},{12,14},{14,12},{16,18},{18,... | collective-permute-start | bytes 786440 | tf_op jit(solution)/shard_map/ppermute | solution.py:24
  3.0 10.8 %collective-permute-start.3 = (f32[512,128]{1,0:T(8,128)S(1)}, f32[512,128]{1,0:T(8,128)S(1)}, u32[]{:S(2)}, u32[]{:S(2)}) collective-permute-start(f32[512,128]{1,0:T(8,128)S(1)} %maximum_bitcast_fusion.refs_1_), channel_id=1, source_target_pairs={{0,1},{1,0},{2,3},{3,2},{4,5},{5,4},{6,7},{7,6},{8,9},{9,8},{10,11... | collective-permute-start | bytes 786440 | tf_op jit(solution)/shard_map/ppermute | solution.py:24
  5.5 11.3 %collective-permute-start.1 = (f32[512,128]{1,0:T(8,128)S(1)}, f32[512,128]{1,0:T(8,128)S(1)}, u32[]{:S(2)}, u32[]{:S(2)}) collective-permute-start(f32[512,128]{1,0:T(8,128)S(1)} %maximum_bitcast_fusion.refs_1_), channel_id=1, source_target_pairs={{0,4},{2,6},{4,8},{6,10},{8,12},{10,14},{12,16},{14,18},{16,20},{1... | collective-permute-start | bytes 786440 | tf_op jit(solution)/shard_map/ppermute | solution.py:24
  13.1 12.4 %collective-permute-start.2 = (f32[512,128]{1,0:T(8,128)S(1)}, f32[512,128]{1,0:T(8,128)S(1)}, u32[]{:S(2)}, u32[]{:S(2)}) collective-permute-start(f32[512,128]{1,0:T(8,128)S(1)} %maximum_bitcast_fusion.refs_1_), channel_id=1, source_target_pairs={{0,28},{2,30},{4,0},{6,2},{8,4},{10,6},{12,8},{14,10},{16,12},{18,... | collective-permute-start | bytes 786440 | tf_op jit(solution)/shard_map/ppermute | solution.py:24
  25.6 3.1 %collective-permute-start.4 = (f32[512,128]{1,0:T(8,128)S(1)}, f32[512,128]{1,0:T(8,128)S(1)}, u32[]{:S(2)}, u32[]{:S(2)}) collective-permute-start(f32[512,128]{1,0:T(8,128)S(1)} %broadcast_select_fusion), channel_id=1, source_target_pairs={{0,2},{2,0},{4,6},{6,4},{8,10},{10,8},{12,14},{14,12},{16,18},{18,... | collective-permute-start | bytes 786440 | tf_op jit(solution)/shard_map/ppermute | solution.py:24
  32.1 5.7 %collective-permute-start.5 = (f32[384,128]{1,0:T(8,128)S(1)}, f32[384,128]{1,0:T(8,128)S(1)}, u32[]{:S(2)}, u32[]{:S(2)}) collective-permute-start(f32[384,128]{1,0:T(8,128)S(1)} %bitcast.15), channel_id=1, source_target_pairs={{0,1},{1,0},{2,3},{3,2},{4,5},{5,4},{6,7},{7,6},{8,9},{9,8},{10,11... | collective-permute-start | bytes 589832 | tf_op jit(solution)/shard_map/ppermute | solution.py:24

commit v2 on v0

--- a/solution.py
+++ b/solution.py
@@ -230,7 +230,14 @@
         for u in range(HALF):
             products(0, u, first_half)
         charge[...] = charge_next[...]
-        lax.fori_loop(0, (listed + GROUP - 1) // GROUP, turn, 0)
+        full = (listed + HALF - 1) // GROUP
+        lax.fori_loop(0, full, turn, 0)
+
+        @pl.when(listed > full * GROUP)
+        def _():
+            sums = [add_up(u, weights(u, first_half)) for u in range(HALF)]
+            for u in range(HALF):
+                total[tile_rows(target_of(full, u), 2 * ROWS), :] += sums[u]
 
 
 def finish(targets, centres, totals, out_ref):
@@ -279,8 +286,8 @@
     near = (run == REACH) | (run == side_of_partner())
     kind = jnp.where(
         mine,
-        jnp.where(near, 0, 4),
-        jnp.where(near | (run == 0), 1, jnp.where(run == 2 * REACH, 2, 3)),
+        jnp.where(near, 0, jnp.where(run == 0, 5, 4)),
+        jnp.where(near, 1, jnp.where(run == 0, 6, jnp.where(run == 2 * REACH, 2, 3))),
     )
     kind = jnp.where(entry < number, kind, CLASSES - 1)
     member = jnp.where(lax.broadcasted_iota(jnp.int32, (CLASSES, length), 0) == kind, 1.0, 0.0)
@@ -347,7 +354,7 @@
     run_class(lists, window, state, scratch)
 
 
-def near_kernel(sorted_list, live, partner, below, *refs, members, length):
+def near_kernel(sorted_list, live, partner, *refs, members, length):
     others, refs = refs[: members - 1], refs[members - 1 :]
     targets, features, centres, total = state = refs[:4]
     window, near_rows, tilt_rows, lists, sems = refs[4:9]
@@ -356,12 +363,26 @@
     blocks = live.shape[0] // ROWS
     window[pl.ds(REACH * blocks * ROWS, blocks * ROWS), :] = live[...]
     put_tiles(window, side_of_partner() * blocks, partner, length)
-    put_tiles(window, 0, below, length)
     for r, other in enumerate(others):
         put_tiles(targets, r * blocks, other, length)
     prepare_targets(state, near_rows, tilt_rows)
     to_scalars.wait()
     run_class(lists, window, state, scratch)
+
+
+def below_kernel(sorted_list, below, live, own_features, own_centres, *refs, length):
+    targets, features, centres, total, own_total = refs[:5]
+    window, lists, sems, own_lists, own_sems = refs[5:10]
+    scratch = refs[10:]
+    to_scalars = read_list(6, sorted_list, lists, sems)
+    own_to_scalars = read_list(5, sorted_list, own_lists, own_sems)
+    total[...] = jnp.zeros_like(total)
+    own_total[...] = jnp.zeros_like(own_total)
+    put_tiles(window, 0, below, length)
+    to_scalars.wait()
+    run_class(lists, window, (targets, features, centres, total), scratch)
+    own_to_scalars.wait()
+    run_class(own_lists, window, (live, own_features, own_centres, own_total), scratch)
 
 
 def single_kernel(sorted_list, tiles, targets, features, centres, *refs, kind, run, length):
@@ -375,9 +396,9 @@
 
 
 def far_kernel(sorted_list, below, above, crossed, *refs, length):
-    targets, features, centres, near_total, middle_total = refs[:5]
-    window, out_ref, total, lists, sems = refs[5:10]
-    scratch = refs[10:]
+    targets, features, centres, near_total, below_total, middle_total = refs[:6]
+    window, out_ref, total, lists, sems = refs[6:11]
+    scratch = refs[11:]
     state = (targets, features, centres, total)
     to_scalars = read_list(3, sorted_list, lists, sems)
     blocks = below.shape[0] // ROWS
@@ -387,16 +408,16 @@
     total[...] = jnp.zeros_like(total)
     to_scalars.wait()
     run_class(lists, window, state, scratch)
-    finish(targets, centres, (near_total, middle_total, total), out_ref)
+    finish(targets, centres, (near_total, below_total, middle_total, total), out_ref)
 
 
 def last_kernel(sorted_list, window, own, features, centres, *refs):
-    home_total, out_ref, total, lists, sems = refs[:5]
+    home_total, below_total, out_ref, total, lists, sems = refs[:6]
     to_scalars = read_list(4, sorted_list, lists, sems)
     total[...] = jnp.zeros_like(total)
     to_scalars.wait()
-    run_class(lists, window, (own, features, centres, total), refs[5:])
-    finish(own, centres, (home_total, total), out_ref)
+    run_class(lists, window, (own, features, centres, total), refs[6:])
+    finish(own, centres, (home_total, below_total, total), out_ref)
 
 
 def section_kernel(own, sums, *refs):
@@ -488,12 +509,20 @@
     other_state = list(call(
         lambda *refs: near_kernel(*refs, members=members, length=length),
         "near_pairs",
-        (lists, live, partner, below, *others),
+        (lists, live, partner, *others),
         other_shapes,
         [window_scratch] + feature_rows + list_scratch + scratch,
         flops=NEAR_FLOPS,
     ))
-    above, other_state[3] = lax.optimization_barrier((above, other_state[3]))
+    below_total, below_own_total = call(
+        lambda *refs: below_kernel(*refs, length=length),
+        "below_pairs",
+        (lists, below, live, *own_state[:2], *other_state[:3]),
+        [other_shapes[3], own_shapes[3]],
+        [pltpu.VMEM(own.shape, jnp.float32)] + 2 * list_scratch + scratch,
+        flops=HOME_FLOPS,
+    )
+    above, below_total = lax.optimization_barrier((above, below_total))
     crossed = moved(jnp.where(shard % 2 == 0, above, below), "blk", to_other_core)
     (middle_total,) = call(
         lambda *refs: single_kernel(*refs, kind=2, run=2 * REACH, length=length),
@@ -507,7 +536,7 @@
     window, away_sums = call(
         lambda *refs: far_kernel(*refs, length=length),
         "far_pairs",
-        (lists, below, above, crossed, *other_state, middle_total),
+        (lists, below, above, crossed, *other_state, below_total, middle_total),
         [window_shape, f32(members - 1, 6 * blocks, BLOCK)],
         [pltpu.VMEM(other_shapes[3].shape, jnp.float32)] + list_scratch + scratch,
         flops=FAR_FLOPS,
@@ -519,7 +548,7 @@
     (sums,) = call(
         last_kernel,
         "last_pairs",
-        (lists, window, live, *own_state),
+        (lists, window, live, *own_state, below_own_total),
         [f32(1, 6 * blocks, BLOCK)],
         [pltpu.VMEM(own_shapes[3].shape, jnp.float32)] + list_scratch + scratch,
         flops=FAR_FLOPS,

time: 38 us -> 35.9 us (0.945); the launches traced: 37.8 us -> 35.2 us
  Pallas kernels: 25 us -> 16.4 us
  waiting for transfers between devices: 2.6 us -> 5.84 us
  starting transfers between devices: 6.96 us -> 9.79 us
    pallas_call x6 -> x7, Pallas kernels: 25 us -> 16.4 us  [call(): pl.pallas_call(kernel, out_shape=outputs, in_specs=[smem if value.dtype =...]
    ppermute x6, waiting for transfers between devices: 2.6 us -> 5.84 us  [moved(): return lax.ppermute(value, axis, pairs)]
    ppermute x6, starting transfers between devices: 6.96 us -> 9.79 us  [moved(): return lax.ppermute(value, axis, pairs)]
  transfers between devices with their start and end apart: 6 -> 6, of which waited for: 1 -> 3; matrix products, arithmetic and copies ran while one was open for 0% -> 0% of each run, Pallas kernels for 54% -> 37%
where the time goes in v2:
time: 35.9 us; the launch traced here: 35.2 us
  Pallas kernels  16.4 us (46%)
  starting transfers between devices  9.79 us (27%)
  waiting for transfers between devices  5.84 us (16%)
  other arithmetic  1.86 us (5%)
  between operations  1.36 us (4%)
    pallas_call x7, Pallas kernels, call(): pl.pallas_call(kernel, out_shape=outputs, in_specs=[smem if value.dtype =...  16.4 us
    ppermute x6, starting transfers between devices, moved(): return lax.ppermute(value, axis, pairs)  9.79 us
    ppermute x6, waiting for transfers between devices, moved(): return lax.ppermute(value, axis, pairs)  5.84 us
    reshape x1, other arithmetic, shards(): own = own.reshape(blocks * ROWS, BLOCK)  1.11 us
    convert_element_type x1, other arithmetic, shards(): listed = sum(rows).astype(jnp.float32).reshape(blocks, 1, BLOCK)  0.72 us
  transfers between devices with their start and end apart: 6, of which 3 were waited for; matrix products, arithmetic and copies ran while one was open for 0% of the time, Pallas kernels for 37%

profile of v2, /device:TPU:0, one launch (start us, length us, event | category | flops | bytes accessed | tf_op | source)
XLA Modules:
  0.0 35.2 jit_solution(6890380665617050392)
XLA Ops:
  0.6 0.7 %add_convert_fusion = f32[8192]{0:T(1024)S(1)} fusion(s32[64]{0:T(128)} %param.10, s32[256]{0:T(256)} %bitcast.20, s32[256]{0:T(256)} %bitcast.21), kind=kLoop, calls=%fused_computation.2 | loop fusion | flops 24576 | bytes 35072 | tf_op jit(solution)/shard_map/convert_element_type | solution.py:470
  1.4 1.1 %maximum_bitcast_fusion.refs_1_ = f32[512,128]{1,0:T(8,128)S(1)} fusion(f32[64,1,128]{2,1,0:T(1,128)S(1)} %bitcast.16, f32[64,1,128]{2,1,0:T(1,128)} %bitcast.19, f32[64,3,128]{2,1,0:T(4,128)} %bitcast.17, f32[64,3,128]{2,1,0:T(4,128)} %bitcast.18), kind=kLoop, calls=%fused_computation | loop fusion | flops 196608 | bytes 524288 | tf_op jit(solution)/shard_map/reshape | solution.py:472
  2.5 0.5 %collective-permute-start = (f32[512,128]{1,0:T(8,128)S(1)}, f32[512,128]{1,0:T(8,128)S(1)}, u32[]{:S(2)}, u32[]{:S(2)}) collective-permute-start(f32[512,128]{1,0:T(8,128)S(1)} %maximum_bitcast_fusion.refs_1_), channel_id=1, source_target_pairs={{0,2},{2,0},{4,6},{6,4},{8,10},{10,8},{12,14},{14,12},{16,18},{18,... | collective-permute-start | bytes 786440 | tf_op jit(solution)/shard_map/ppermute | solution.py:24
  3.0 2.6 %collective-permute-start.3 = (f32[512,128]{1,0:T(8,128)S(1)}, f32[512,128]{1,0:T(8,128)S(1)}, u32[]{:S(2)}, u32[]{:S(2)}) collective-permute-start(f32[512,128]{1,0:T(8,128)S(1)} %maximum_bitcast_fusion.refs_1_), channel_id=1, source_target_pairs={{0,1},{1,0},{2,3},{3,2},{4,5},{5,4},{6,7},{7,6},{8,9},{9,8},{10,11... | collective-permute-start | bytes 786440 | tf_op jit(solution)/shard_map/ppermute | solution.py:24
  5.5 1.5 %collective-permute-start.1 = (f32[512,128]{1,0:T(8,128)S(1)}, f32[512,128]{1,0:T(8,128)S(1)}, u32[]{:S(2)}, u32[]{:S(2)}) collective-permute-start(f32[512,128]{1,0:T(8,128)S(1)} %maximum_bitcast_fusion.refs_1_), channel_id=1, source_target_pairs={{0,4},{2,6},{4,8},{6,10},{8,12},{10,14},{12,16},{14,18},{16,20},{1... | collective-permute-start | bytes 786440 | tf_op jit(solution)/shard_map/ppermute | solution.py:24
  7.7 0.0 collective-permute-done.refs_2_
  7.7 2.7 %home_pairs.1 = (s32[7,8,128]{2,1,0:T(8,128)S(1)}, f32[512,128]{1,0:T(8,128)S(1)}, bf16[64,48,256]{2,1,0:T(8,128)(2,1)S(1)}, f32[512,128]{1,0:T(8,128)S(1)}, f32[1024,128]{1,0:T(8,128)S(1)}) custom-call(s32[1]{0:T(128)S(6)} %copy.13.refs_0_, f32[512,128]{1,0:T(8,128)S(1)} %maximum_bitcast_fusion.refs_1_, f32[512,128]{1,0:T(8,128)S(1)} %collective-permute-done.refs_2_), custom_call_target="tpu_custom_call" | custom-call | flops 10000000000 | tf_op jit(solution)/shard_map/home_pairs/pallas_call | solution.py:442
  10.5 3.3 %collective-permute-start.2 = (f32[512,128]{1,0:T(8,128)S(1)}, f32[512,128]{1,0:T(8,128)S(1)}, u32[]{:S(2)}, u32[]{:S(2)}) collective-permute-start(f32[512,128]{1,0:T(8,128)S(1)} %maximum_bitcast_fusion.refs_1_), channel_id=1, source_target_pairs={{0,28},{2,30},{4,0},{6,2},{8,4},{10,6},{12,8},{14,10},{16,12},{18,... | collective-permute-start | bytes 786440 | tf_op jit(solution)/shard_map/ppermute | solution.py:24
  13.7 0.0 collective-permute-done.3.refs_3_
  13.7 3.0 %near_pairs.1 = (f32[512,128]{1,0:T(8,128)S(1)}, bf16[64,48,256]{2,1,0:T(8,128)(2,1)S(1)}, f32[512,128]{1,0:T(8,128)S(1)}, f32[1024,128]{1,0:T(8,128)S(1)}) custom-call(s32[7,8,128]{2,1,0:T(8,128)S(1)} %get-tuple-element.25.refs_0_.sorted_list, f32[512,128]{1,0:T(8,128)S(1)} %get-tuple-element.23.refs_1_.refs_2_.own, ...), custom_call_target="tpu_custom_call" | custom-call | flops 10000000000 | tf_op jit(solution)/shard_map/near_pairs/pallas_call | solution.py:442
  16.8 0.1 collective-permute-done.1.refs_1_
  16.8 2.6 %below_pairs.1 = (f32[1024,128]{1,0:T(8,128)S(1)}, f32[1024,128]{1,0:T(8,128)S(1)}) custom-call(s32[7,8,128]{2,1,0:T(8,128)S(1)} %get-tuple-element.25.refs_0_.sorted_list, f32[512,128]{1,0:T(8,128)S(1)} %collective-permute-done.1.refs_1_, f32[512,128]{1,0:T(8,128)S(1)} %get-tuple-element.23.refs_1_.refs_2_.own, ...), custom_call_target="tpu_custom_call" | custom-call | flops 10000000000 | tf_op jit(solution)/shard_map/below_pairs/pallas_call | solution.py:442
  19.5 2.8 %collective-permute-done.2.refs_1_.refs_2_ = f32[512,128]{1,0:T(8,128)S(1)} collective-permute-done((f32[512,128]{1,0:T(8,128)S(1)}, f32[512,128]{1,0:T(8,128)S(1)}, u32[]{:S(2)}, u32[]{:S(2)}) %collective-permute-start.2) | collective-permute-done | bytes 262176 | tf_op jit(solution)/shard_map/ppermute | solution.py:24
  22.3 0.6 %collective-permute-start.4 = (f32[512,128]{1,0:T(8,128)S(1)}, f32[512,128]{1,0:T(8,128)S(1)}, u32[]{:S(2)}, u32[]{:S(2)}) collective-permute-start(f32[512,128]{1,0:T(8,128)S(1)} %broadcast_select_fusion), channel_id=1, source_target_pairs={{0,2},{2,0},{4,6},{6,4},{8,10},{10,8},{12,14},{14,12},{16,18},{18,... | collective-permute-start | bytes 786440 | tf_op jit(solution)/shard_map/ppermute | solution.py:24
  22.9 1.7 %middle_pairs.1.refs_9_ = f32[1024,128]{1,0:T(8,128)S(1)} custom-call(s32[7,8,128]{2,1,0:T(8,128)S(1)} %get-tuple-element.25.refs_0_.sorted_list, f32[512,128]{1,0:T(8,128)S(1)} %collective-permute-done.2.refs_1_.refs_2_, f32[512,128]{1,0:T(8,128)S(1)} %get-tuple-element.29.refs_5_.refs_2_.refs_4_, ...), custom_call_target="tpu_custom_call" | custom-call | flops 10000000000 | tf_op jit(solution)/shard_map/middle_pairs/pallas_call | solution.py:442
  24.6 0.0 collective-permute-done.4.refs_3_
  24.6 2.3 %far_pairs.1 = (f32[2560,128]{1,0:T(8,128)S(1)}, f32[1,384,128]{2,1,0:T(8,128)S(1)}) custom-call(s32[7,8,128]{2,1,0:T(8,128)S(1)} %get-tuple-element.25.refs_0_.sorted_list, f32[512,128]{1,0:T(8,128)S(1)} %collective-permute-done.1.refs_1_, f32[512,128]{1,0:T(8,128)S(1)} %collective-permute-done.2.refs_1_.refs_2_, ...), custom_call_target="tpu_custom_call" | custom-call | flops 10000000000 | tf_op jit(solution)/shard_map/far_pairs/pallas_call | solution.py:442
  26.9 1.3 %collective-permute-start.5 = (f32[384,128]{1,0:T(8,128)S(1)}, f32[384,128]{1,0:T(8,128)S(1)}, u32[]{:S(2)}, u32[]{:S(2)}) collective-permute-start(f32[384,128]{1,0:T(8,128)S(1)} %bitcast.15), channel_id=1, source_target_pairs={{0,1},{1,0},{2,3},{3,2},{4,5},{5,4},{6,7},{7,6},{8,9},{9,8},{10,11... | collective-permute-start | bytes 589832 | tf_op jit(solution)/shard_map/ppermute | solution.py:24
  28.2 2.9 %last_pairs.1 = f32[1,384,128]{2,1,0:T(8,128)S(1)} custom-call(s32[7,8,128]{2,1,0:T(8,128)S(1)} %get-tuple-element.25.refs_0_.sorted_list, f32[2560,128]{1,0:T(8,128)S(1)} %get-tuple-element.38.window, f32[512,128]{1,0:T(8,128)S(1)} %get-tuple-element.23.refs_1_.refs_2_.own, bf16[64,48,256]{2,1,0:T(8,128)(2,1)S(1)} %get-tuple-element.27.refs_3_.features, ...), custom_call_target="tpu_custom_call" | custom-call | flops 10000000000 | tf_op jit(solution)/shard_map/last_pairs/pallas_call | solution.py:442
  31.2 3.0 %collective-permute-done.5.refs_0_ = f32[384,128]{1,0:T(8,128)S(1)} collective-permute-done((f32[384,128]{1,0:T(8,128)S(1)}, f32[384,128]{1,0:T(8,128)S(1)}, u32[]{:S(2)}, u32[]{:S(2)}) %collective-permute-start.5) | collective-permute-done | bytes 196640 | tf_op jit(solution)/shard_map/ppermute | solution.py:24
  34.1 1.1 %section.1 = (f32[3,8192]{1,0:T(4,128)}, f32[3,8192]{1,0:T(4,128)}, f32[3,8192]{1,0:T(4,128)}, f32[3,8192]{1,0:T(4,128)}) custom-call(f32[512,128]{1,0:T(8,128)S(1)} %get-tuple-element.23.refs_1_.refs_2_.own, f32[384,128]{1,0:T(8,128)S(1)} %bitcast.14, f32[384,128]{1,0:T(8,128)S(1)} %collective-permute-done.5.refs_0_), custom_call_target="tpu_custom_call" | custom-call | tf_op jit(solution)/shard_map/section/pallas_call | solution.py:442
  (1 shorter events, 0.0 us)
Async XLA Ops:
  2.5 5.3 %collective-permute-start = (f32[512,128]{1,0:T(8,128)S(1)}, f32[512,128]{1,0:T(8,128)S(1)}, u32[]{:S(2)}, u32[]{:S(2)}) collective-permute-start(f32[512,128]{1,0:T(8,128)S(1)} %maximum_bitcast_fusion.refs_1_), channel_id=1, source_target_pairs={{0,2},{2,0},{4,6},{6,4},{8,10},{10,8},{12,14},{14,12},{16,18},{18,... | collective-permute-start | bytes 786440 | tf_op jit(solution)/shard_map/ppermute | solution.py:24
  3.0 10.8 %collective-permute-start.3 = (f32[512,128]{1,0:T(8,128)S(1)}, f32[512,128]{1,0:T(8,128)S(1)}, u32[]{:S(2)}, u32[]{:S(2)}) collective-permute-start(f32[512,128]{1,0:T(8,128)S(1)} %maximum_bitcast_fusion.refs_1_), channel_id=1, source_target_pairs={{0,1},{1,0},{2,3},{3,2},{4,5},{5,4},{6,7},{7,6},{8,9},{9,8},{10,11... | collective-permute-start | bytes 786440 | tf_op jit(solution)/shard_map/ppermute | solution.py:24
  5.5 11.3 %collective-permute-start.1 = (f32[512,128]{1,0:T(8,128)S(1)}, f32[512,128]{1,0:T(8,128)S(1)}, u32[]{:S(2)}, u32[]{:S(2)}) collective-permute-start(f32[512,128]{1,0:T(8,128)S(1)} %maximum_bitcast_fusion.refs_1_), channel_id=1, source_target_pairs={{0,4},{2,6},{4,8},{6,10},{8,12},{10,14},{12,16},{14,18},{16,20},{1... | collective-permute-start | bytes 786440 | tf_op jit(solution)/shard_map/ppermute | solution.py:24
  10.5 11.8 %collective-permute-start.2 = (f32[512,128]{1,0:T(8,128)S(1)}, f32[512,128]{1,0:T(8,128)S(1)}, u32[]{:S(2)}, u32[]{:S(2)}) collective-permute-start(f32[512,128]{1,0:T(8,128)S(1)} %maximum_bitcast_fusion.refs_1_), channel_id=1, source_target_pairs={{0,28},{2,30},{4,0},{6,2},{8,4},{10,6},{12,8},{14,10},{16,12},{18,... | collective-permute-start | bytes 786440 | tf_op jit(solution)/shard_map/ppermute | solution.py:24
  22.3 2.3 %collective-permute-start.4 = (f32[512,128]{1,0:T(8,128)S(1)}, f32[512,128]{1,0:T(8,128)S(1)}, u32[]{:S(2)}, u32[]{:S(2)}) collective-permute-start(f32[512,128]{1,0:T(8,128)S(1)} %broadcast_select_fusion), channel_id=1, source_target_pairs={{0,2},{2,0},{4,6},{6,4},{8,10},{10,8},{12,14},{14,12},{16,18},{18,... | collective-permute-start | bytes 786440 | tf_op jit(solution)/shard_map/ppermute | solution.py:24
  26.9 7.2 %collective-permute-start.5 = (f32[384,128]{1,0:T(8,128)S(1)}, f32[384,128]{1,0:T(8,128)S(1)}, u32[]{:S(2)}, u32[]{:S(2)}) collective-permute-start(f32[384,128]{1,0:T(8,128)S(1)} %bitcast.15), channel_id=1, source_target_pairs={{0,1},{1,0},{2,3},{3,2},{4,5},{5,4},{6,7},{7,6},{8,9},{9,8},{10,11... | collective-permute-start | bytes 589832 | tf_op jit(solution)/shard_map/ppermute | solution.py:24

commit v3 on v2

--- a/solution.py
+++ b/solution.py
@@ -287,7 +287,7 @@
     kind = jnp.where(
         mine,
         jnp.where(near, 0, jnp.where(run == 0, 5, 4)),
-        jnp.where(near, 1, jnp.where(run == 0, 6, jnp.where(run == 2 * REACH, 2, 3))),
+        jnp.where(near, 1, jnp.where(run == 0, 2, 3)),
     )
     kind = jnp.where(entry < number, kind, CLASSES - 1)
     member = jnp.where(lax.broadcasted_iota(jnp.int32, (CLASSES, length), 0) == kind, 1.0, 0.0)
@@ -370,45 +370,28 @@
     run_class(lists, window, state, scratch)
 
 
-def below_kernel(sorted_list, below, live, own_features, own_centres, *refs, length):
-    targets, features, centres, total, own_total = refs[:5]
-    window, lists, sems, own_lists, own_sems = refs[5:10]
-    scratch = refs[10:]
-    to_scalars = read_list(6, sorted_list, lists, sems)
-    own_to_scalars = read_list(5, sorted_list, own_lists, own_sems)
-    total[...] = jnp.zeros_like(total)
-    own_total[...] = jnp.zeros_like(own_total)
-    put_tiles(window, 0, below, length)
-    to_scalars.wait()
-    run_class(lists, window, (targets, features, centres, total), scratch)
-    own_to_scalars.wait()
-    run_class(own_lists, window, (live, own_features, own_centres, own_total), scratch)
-
-
-def single_kernel(sorted_list, tiles, targets, features, centres, *refs, kind, run, length):
+def single_kernel(sorted_list, tiles, targets, features, centres, *refs, kind, length):
     total, window, lists, sems = refs[:4]
     to_scalars = read_list(kind, sorted_list, lists, sems)
     total[...] = jnp.zeros_like(total)
     put_tiles(window, 0, tiles, length)
     to_scalars.wait()
-    window = shifted_window(window, run * (tiles.shape[0] // ROWS))
     run_class(lists, window, (targets, features, centres, total), refs[4:])
 
 
-def far_kernel(sorted_list, below, above, crossed, *refs, length):
-    targets, features, centres, near_total, below_total, middle_total = refs[:6]
-    window, out_ref, total, lists, sems = refs[6:11]
-    scratch = refs[11:]
+def far_kernel(sorted_list, above, crossed, *refs, length):
+    targets, features, centres, near_total, below_total = refs[:5]
+    window, out_ref, total, lists, sems = refs[5:10]
+    scratch = refs[10:]
     state = (targets, features, centres, total)
     to_scalars = read_list(3, sorted_list, lists, sems)
-    blocks = below.shape[0] // ROWS
-    put_tiles(window, 0, below, length)
+    blocks = above.shape[0] // ROWS
     put_tiles(window, 2 * REACH * blocks, above, length)
     put_tiles(window, (2 * REACH - side_of_partner()) * blocks, crossed, length)
     total[...] = jnp.zeros_like(total)
     to_scalars.wait()
     run_class(lists, window, state, scratch)
-    finish(targets, centres, (near_total, below_total, middle_total, total), out_ref)
+    finish(targets, centres, (near_total, below_total, total), out_ref)
 
 
 def last_kernel(sorted_list, window, own, features, centres, *refs):
@@ -514,29 +497,29 @@
         [window_scratch] + feature_rows + list_scratch + scratch,
         flops=NEAR_FLOPS,
     ))
-    below_total, below_own_total = call(
-        lambda *refs: below_kernel(*refs, length=length),
+    (below_total,) = call(
+        lambda *refs: single_kernel(*refs, kind=2, length=length),
         "below_pairs",
-        (lists, below, live, *own_state[:2], *other_state[:3]),
-        [other_shapes[3], own_shapes[3]],
-        [pltpu.VMEM(own.shape, jnp.float32)] + 2 * list_scratch + scratch,
-        flops=HOME_FLOPS,
-    )
-    above, below_total = lax.optimization_barrier((above, below_total))
-    crossed = moved(jnp.where(shard % 2 == 0, above, below), "blk", to_other_core)
-    (middle_total,) = call(
-        lambda *refs: single_kernel(*refs, kind=2, run=2 * REACH, length=length),
-        "middle_pairs",
-        (lists, above, *other_state[:3]),
+        (lists, below, *other_state[:3]),
         [other_shapes[3]],
         [pltpu.VMEM(own.shape, jnp.float32)] + list_scratch + scratch,
         flops=HOME_FLOPS,
     )
-    crossed, middle_total = lax.optimization_barrier((crossed, middle_total))
+    above, below_total = lax.optimization_barrier((above, below_total))
+    crossed = moved(jnp.where(shard % 2 == 0, above, below), "blk", to_other_core)
+    (below_own_total,) = call(
+        lambda *refs: single_kernel(*refs, kind=5, length=length),
+        "below_own_pairs",
+        (lists, below, live, *own_state[:2]),
+        [own_shapes[3]],
+        [pltpu.VMEM(own.shape, jnp.float32)] + list_scratch + scratch,
+        flops=HOME_FLOPS,
+    )
+    crossed, below_own_total = lax.optimization_barrier((crossed, below_own_total))
     window, away_sums = call(
         lambda *refs: far_kernel(*refs, length=length),
         "far_pairs",
-        (lists, below, above, crossed, *other_state, below_total, middle_total),
+        (lists, above, crossed, *other_state, below_total),
         [window_shape, f32(members - 1, 6 * blocks, BLOCK)],
         [pltpu.VMEM(other_shapes[3].shape, jnp.float32)] + list_scratch + scratch,
         flops=FAR_FLOPS,

time: 35.9 us -> 35.7 us (level); the launches traced: 35.2 us -> 35.5 us
  starting transfers between devices: 9.79 us -> 11.4 us
  Pallas kernels: 16.4 us -> 15.1 us
    ppermute x6, starting transfers between devices: 9.79 us -> 11.4 us  [moved(): return lax.ppermute(value, axis, pairs)]
    pallas_call x7, Pallas kernels: 16.4 us -> 15.1 us  [call(): pl.pallas_call(kernel, out_shape=outputs, in_specs=[smem if value.dtype =...]
  transfers between devices with their start and end apart: 6 -> 6, of which waited for: 3 -> 2; matrix products, arithmetic and copies ran while one was open for 0% -> 0% of each run, Pallas kernels for 37% -> 33%
where the time goes in v3:
time: 35.7 us; the launch traced here: 35.5 us
  Pallas kernels  15.1 us (42%)
  starting transfers between devices  11.4 us (32%)
  waiting for transfers between devices  5.75 us (16%)
  other arithmetic  1.86 us (5%)
  between operations  1.36 us (4%)
    pallas_call x7, Pallas kernels, call(): pl.pallas_call(kernel, out_shape=outputs, in_specs=[smem if value.dtype =...  15.1 us
    ppermute x6, starting transfers between devices, moved(): return lax.ppermute(value, axis, pairs)  11.4 us
    ppermute x6, waiting for transfers between devices, moved(): return lax.ppermute(value, axis, pairs)  5.75 us
    reshape x1, other arithmetic, shards(): own = own.reshape(blocks * ROWS, BLOCK)  1.11 us
    convert_element_type x1, other arithmetic, shards(): listed = sum(rows).astype(jnp.float32).reshape(blocks, 1, BLOCK)  0.72 us
  transfers between devices with their start and end apart: 6, of which 2 were waited for; matrix products, arithmetic and copies ran while one was open for 0% of the time, Pallas kernels for 33%

profile of v3, /device:TPU:0, one launch (start us, length us, event | category | flops | bytes accessed | tf_op | source)
XLA Modules:
  0.0 35.5 jit_solution(10870744115788601445)
XLA Ops:
  0.6 0.7 %add_convert_fusion = f32[8192]{0:T(1024)S(1)} fusion(s32[64]{0:T(128)} %param.10, s32[256]{0:T(256)} %bitcast.20, s32[256]{0:T(256)} %bitcast.21), kind=kLoop, calls=%fused_computation.2 | loop fusion | flops 24576 | bytes 35072 | tf_op jit(solution)/shard_map/convert_element_type | solution.py:453
  1.4 1.1 %maximum_bitcast_fusion.refs_1_ = f32[512,128]{1,0:T(8,128)S(1)} fusion(f32[64,1,128]{2,1,0:T(1,128)S(1)} %bitcast.16, f32[64,1,128]{2,1,0:T(1,128)} %bitcast.19, f32[64,3,128]{2,1,0:T(4,128)} %bitcast.17, f32[64,3,128]{2,1,0:T(4,128)} %bitcast.18), kind=kLoop, calls=%fused_computation | loop fusion | flops 196608 | bytes 524288 | tf_op jit(solution)/shard_map/reshape | solution.py:455
  2.5 0.5 %collective-permute-start = (f32[512,128]{1,0:T(8,128)S(1)}, f32[512,128]{1,0:T(8,128)S(1)}, u32[]{:S(2)}, u32[]{:S(2)}) collective-permute-start(f32[512,128]{1,0:T(8,128)S(1)} %maximum_bitcast_fusion.refs_1_), channel_id=1, source_target_pairs={{0,2},{2,0},{4,6},{6,4},{8,10},{10,8},{12,14},{14,12},{16,18},{18,... | collective-permute-start | bytes 786440 | tf_op jit(solution)/shard_map/ppermute | solution.py:24
  3.0 2.6 %collective-permute-start.3 = (f32[512,128]{1,0:T(8,128)S(1)}, f32[512,128]{1,0:T(8,128)S(1)}, u32[]{:S(2)}, u32[]{:S(2)}) collective-permute-start(f32[512,128]{1,0:T(8,128)S(1)} %maximum_bitcast_fusion.refs_1_), channel_id=1, source_target_pairs={{0,1},{1,0},{2,3},{3,2},{4,5},{5,4},{6,7},{7,6},{8,9},{9,8},{10,11... | collective-permute-start | bytes 786440 | tf_op jit(solution)/shard_map/ppermute | solution.py:24
  5.5 1.5 %collective-permute-start.2 = (f32[512,128]{1,0:T(8,128)S(1)}, f32[512,128]{1,0:T(8,128)S(1)}, u32[]{:S(2)}, u32[]{:S(2)}) collective-permute-start(f32[512,128]{1,0:T(8,128)S(1)} %maximum_bitcast_fusion.refs_1_), channel_id=1, source_target_pairs={{0,4},{2,6},{4,8},{6,10},{8,12},{10,14},{12,16},{14,18},{16,20},{1... | collective-permute-start | bytes 786440 | tf_op jit(solution)/shard_map/ppermute | solution.py:24
  7.7 0.0 collective-permute-done.refs_2_
  7.7 3.0 %home_pairs.1 = (s32[7,8,128]{2,1,0:T(8,128)S(1)}, f32[512,128]{1,0:T(8,128)S(1)}, bf16[64,48,256]{2,1,0:T(8,128)(2,1)S(1)}, f32[512,128]{1,0:T(8,128)S(1)}, f32[1024,128]{1,0:T(8,128)S(1)}) custom-call(s32[1]{0:T(128)S(6)} %copy.13.refs_0_, f32[512,128]{1,0:T(8,128)S(1)} %maximum_bitcast_fusion.refs_1_, f32[512,128]{1,0:T(8,128)S(1)} %collective-permute-done.refs_2_), custom_call_target="tpu_custom_call" | custom-call | flops 10000000000 | tf_op jit(solution)/shard_map/home_pairs/pallas_call | solution.py:425
  10.7 5.6 %collective-permute-start.1 = (f32[512,128]{1,0:T(8,128)S(1)}, f32[512,128]{1,0:T(8,128)S(1)}, u32[]{:S(2)}, u32[]{:S(2)}) collective-permute-start(f32[512,128]{1,0:T(8,128)S(1)} %maximum_bitcast_fusion.refs_1_), channel_id=1, source_target_pairs={{0,28},{2,30},{4,0},{6,2},{8,4},{10,6},{12,8},{14,10},{16,12},{18,... | collective-permute-start | bytes 786440 | tf_op jit(solution)/shard_map/ppermute | solution.py:24
  16.3 0.0 collective-permute-done.3.refs_3_
  16.3 2.8 %near_pairs.1 = (f32[512,128]{1,0:T(8,128)S(1)}, bf16[64,48,256]{2,1,0:T(8,128)(2,1)S(1)}, f32[512,128]{1,0:T(8,128)S(1)}, f32[1024,128]{1,0:T(8,128)S(1)}) custom-call(s32[7,8,128]{2,1,0:T(8,128)S(1)} %get-tuple-element.23.refs_0_.sorted_list, f32[512,128]{1,0:T(8,128)S(1)} %get-tuple-element.21.refs_1_.refs_2_.own, ...), custom_call_target="tpu_custom_call" | custom-call | flops 10000000000 | tf_op jit(solution)/shard_map/near_pairs/pallas_call | solution.py:425
  19.1 0.0 collective-permute-done.2.refs_1_
  19.1 1.7 %below_pairs.1.refs_7_ = f32[1024,128]{1,0:T(8,128)S(1)} custom-call(s32[7,8,128]{2,1,0:T(8,128)S(1)} %get-tuple-element.23.refs_0_.sorted_list, f32[512,128]{1,0:T(8,128)S(1)} %collective-permute-done.2.refs_1_, f32[512,128]{1,0:T(8,128)S(1)} %get-tuple-element.25.refs_2_.refs_3_, bf16[64,48,256]{2,1,0:T(8,128)(2,1)S(1)} %get-tuple-element.26.refs_3_.refs_4_, ...), custom_call_target="tpu_custom_call" | custom-call | flops 10000000000 | tf_op jit(solution)/shard_map/below_pairs/pallas_call | solution.py:425
  20.8 1.5 %collective-permute-done.1.refs_1_ = f32[512,128]{1,0:T(8,128)S(1)} collective-permute-done((f32[512,128]{1,0:T(8,128)S(1)}, f32[512,128]{1,0:T(8,128)S(1)}, u32[]{:S(2)}, u32[]{:S(2)}) %collective-permute-start.1) | collective-permute-done | bytes 262176 | tf_op jit(solution)/shard_map/ppermute | solution.py:24
  22.4 0.1 collective-permute-start.4
  22.5 1.7 %below_own_pairs.1.refs_1_ = f32[1024,128]{1,0:T(8,128)S(1)} custom-call(s32[7,8,128]{2,1,0:T(8,128)S(1)} %get-tuple-element.23.refs_0_.sorted_list, f32[512,128]{1,0:T(8,128)S(1)} %collective-permute-done.2.refs_1_, f32[512,128]{1,0:T(8,128)S(1)} %get-tuple-element.21.refs_1_.refs_2_.own, bf16[64,48,256]{2,1,0:T(8,128)(2,1)S(1)} %get-tuple-element.29.refs_3_.features, ...), custom_call_target="tpu_custom_call" | custom-call | flops 10000000000 | tf_op jit(solution)/shard_map/below_own_pairs/pallas_call | solution.py:425
  24.2 0.0 collective-permute-done.4.refs_2_
  24.2 2.4 %far_pairs.1 = (f32[2560,128]{1,0:T(8,128)S(1)}, f32[1,384,128]{2,1,0:T(8,128)S(1)}) custom-call(s32[7,8,128]{2,1,0:T(8,128)S(1)} %get-tuple-element.23.refs_0_.sorted_list, f32[512,128]{1,0:T(8,128)S(1)} %collective-permute-done.1.refs_1_, f32[512,128]{1,0:T(8,128)S(1)} %collective-permute-done.4.refs_2_, f32[512,128]{1,0:T(8,128)S(1)} %get-tuple-element.25.refs_2_.refs_3_, ...), custom_call_target="tpu_custom_call" | custom-call | flops 10000000000 | tf_op jit(solution)/shard_map/far_pairs/pallas_call | solution.py:425
  26.6 1.2 %collective-permute-start.5 = (f32[384,128]{1,0:T(8,128)S(1)}, f32[384,128]{1,0:T(8,128)S(1)}, u32[]{:S(2)}, u32[]{:S(2)}) collective-permute-start(f32[384,128]{1,0:T(8,128)S(1)} %bitcast.15), channel_id=1, source_target_pairs={{0,1},{1,0},{2,3},{3,2},{4,5},{5,4},{6,7},{7,6},{8,9},{9,8},{10,11... | collective-permute-start | bytes 589832 | tf_op jit(solution)/shard_map/ppermute | solution.py:24
  27.8 2.4 %last_pairs.1 = f32[1,384,128]{2,1,0:T(8,128)S(1)} custom-call(s32[7,8,128]{2,1,0:T(8,128)S(1)} %get-tuple-element.23.refs_0_.sorted_list, f32[2560,128]{1,0:T(8,128)S(1)} %get-tuple-element.34.window, f32[512,128]{1,0:T(8,128)S(1)} %get-tuple-element.21.refs_1_.refs_2_.own, bf16[64,48,256]{2,1,0:T(8,128)(2,1)S(1)} %get-tuple-element.29.refs_3_.features, ...), custom_call_target="tpu_custom_call" | custom-call | flops 10000000000 | tf_op jit(solution)/shard_map/last_pairs/pallas_call | solution.py:425
  30.2 4.2 %collective-permute-done.5.refs_0_ = f32[384,128]{1,0:T(8,128)S(1)} collective-permute-done((f32[384,128]{1,0:T(8,128)S(1)}, f32[384,128]{1,0:T(8,128)S(1)}, u32[]{:S(2)}, u32[]{:S(2)}) %collective-permute-start.5) | collective-permute-done | bytes 196640 | tf_op jit(solution)/shard_map/ppermute | solution.py:24
  34.4 1.1 %section.1 = (f32[3,8192]{1,0:T(4,128)}, f32[3,8192]{1,0:T(4,128)}, f32[3,8192]{1,0:T(4,128)}, f32[3,8192]{1,0:T(4,128)}) custom-call(f32[512,128]{1,0:T(8,128)S(1)} %get-tuple-element.21.refs_1_.refs_2_.own, f32[384,128]{1,0:T(8,128)S(1)} %bitcast.14, f32[384,128]{1,0:T(8,128)S(1)} %collective-permute-done.5.refs_0_), custom_call_target="tpu_custom_call" | custom-call | tf_op jit(solution)/shard_map/section/pallas_call | solution.py:425
  (1 shorter events, 0.0 us)
Async XLA Ops:
  2.5 5.3 %collective-permute-start = (f32[512,128]{1,0:T(8,128)S(1)}, f32[512,128]{1,0:T(8,128)S(1)}, u32[]{:S(2)}, u32[]{:S(2)}) collective-permute-start(f32[512,128]{1,0:T(8,128)S(1)} %maximum_bitcast_fusion.refs_1_), channel_id=1, source_target_pairs={{0,2},{2,0},{4,6},{6,4},{8,10},{10,8},{12,14},{14,12},{16,18},{18,... | collective-permute-start | bytes 786440 | tf_op jit(solution)/shard_map/ppermute | solution.py:24
  3.0 13.3 %collective-permute-start.3 = (f32[512,128]{1,0:T(8,128)S(1)}, f32[512,128]{1,0:T(8,128)S(1)}, u32[]{:S(2)}, u32[]{:S(2)}) collective-permute-start(f32[512,128]{1,0:T(8,128)S(1)} %maximum_bitcast_fusion.refs_1_), channel_id=1, source_target_pairs={{0,1},{1,0},{2,3},{3,2},{4,5},{5,4},{6,7},{7,6},{8,9},{9,8},{10,11... | collective-permute-start | bytes 786440 | tf_op jit(solution)/shard_map/ppermute | solution.py:24
  5.5 13.6 %collective-permute-start.2 = (f32[512,128]{1,0:T(8,128)S(1)}, f32[512,128]{1,0:T(8,128)S(1)}, u32[]{:S(2)}, u32[]{:S(2)}) collective-permute-start(f32[512,128]{1,0:T(8,128)S(1)} %maximum_bitcast_fusion.refs_1_), channel_id=1, source_target_pairs={{0,4},{2,6},{4,8},{6,10},{8,12},{10,14},{12,16},{14,18},{16,20},{1... | collective-permute-start | bytes 786440 | tf_op jit(solution)/shard_map/ppermute | solution.py:24
  10.7 11.6 %collective-permute-start.1 = (f32[512,128]{1,0:T(8,128)S(1)}, f32[512,128]{1,0:T(8,128)S(1)}, u32[]{:S(2)}, u32[]{:S(2)}) collective-permute-start(f32[512,128]{1,0:T(8,128)S(1)} %maximum_bitcast_fusion.refs_1_), channel_id=1, source_target_pairs={{0,28},{2,30},{4,0},{6,2},{8,4},{10,6},{12,8},{14,10},{16,12},{18,... | collective-permute-start | bytes 786440 | tf_op jit(solution)/shard_map/ppermute | solution.py:24
  22.4 1.8 %collective-permute-start.4 = (f32[512,128]{1,0:T(8,128)S(1)}, f32[512,128]{1,0:T(8,128)S(1)}, u32[]{:S(2)}, u32[]{:S(2)}) collective-permute-start(f32[512,128]{1,0:T(8,128)S(1)} %broadcast_select_fusion), channel_id=1, source_target_pairs={{0,2},{2,0},{4,6},{6,4},{8,10},{10,8},{12,14},{14,12},{16,18},{18,... | collective-permute-start | bytes 786440 | tf_op jit(solution)/shard_map/ppermute | solution.py:24
  26.6 7.8 %collective-permute-start.5 = (f32[384,128]{1,0:T(8,128)S(1)}, f32[384,128]{1,0:T(8,128)S(1)}, u32[]{:S(2)}, u32[]{:S(2)}) collective-permute-start(f32[384,128]{1,0:T(8,128)S(1)} %bitcast.15), channel_id=1, source_target_pairs={{0,1},{1,0},{2,3},{3,2},{4,5},{5,4},{6,7},{7,6},{8,9},{9,8},{10,11... | collective-permute-start | bytes 589832 | tf_op jit(solution)/shard_map/ppermute | solution.py:24
